TPU v7x, 32 devices: a whole 2x2x4 slice. The times are simulated.
32 devices in a mesh: seq: 16 (over z, y, core), mlp: 2 (over x).
Axes of the slice: x: 2, y: 2, z: 4, core: 2. Of those that a mesh axis runs over, the one named last changes fastest.
Arguments:
- inputs: bfloat16 [2048, 768], P('seq'), may hold values from -6 to 6
- segments: int32 [2048], P('seq'), may hold values from 0 to 4, as said below
- picks: int32 [1, 256], replicated, may hold values from 0 to 2047, as said below
- gains: float32 [2, 2, 768], replicated, may hold values from 0.5 to 1.5
- router: float32 [768], replicated, may hold values from -0.21875 to 0.21875
- qkv: bfloat16 [2, 3, 768, 768], P(None, None, None, 'mlp'), may hold values from -0.21875 to 0.21875
- proj_out: bfloat16 [2, 768, 768], P(None, 'mlp'), may hold values from -3 to 3
- up: bfloat16 [2, 768, 3072], P(None, None, 'mlp'), may hold values from -0.21875 to 0.21875
- down: bfloat16 [2, 3072, 768], P(None, 'mlp'), may hold values from -0.109375 to 0.109375
- cotangent: bfloat16 [2048, 768], P('seq'), may hold values from -6 to 6
Outputs:
- routed_out: bfloat16 [2048, 768], P('seq')
- dense_out: bfloat16 [2048, 768], P('seq')
- input_grad: float32 [2048, 768], P('seq')
- gains_grad: float32 [2, 2, 768], P(None, None, 'seq')
- router_grad: float32 [768], P('seq')
- qkv_grad: float32 [2, 3, 768, 768], P(None, None, 'seq', 'mlp')
- proj_out_grad: float32 [2, 768, 768], P(None, 'mlp', 'seq')
- up_grad: float32 [2, 768, 3072], P(None, 'seq', 'mlp')
- down_grad: float32 [2, 3072, 768], P(None, 'mlp', 'seq')
Inputs may be any that keep to these rules, and one draw needn't show every extreme that they name: `picks`: each row lists 256 increasing positions of one routing window. Splitting a window into aligned runs of 128 positions, some run of each row holds exactly 128 of them and none holds more. `segments`: document ids never fall along the sequence; every id is used. One document starts within the first 128 tokens and ends within the last 128.
All inputs are finite; a program needn't handle non-finite values.
Results may differ from a plain program's by a relative error of at most 0.018.
Values may be sent and summed in bfloat16 or wider, within the bound.
A program may use at most 128 MiB of HBM per device.

v0:
```python
from functools import partial
import math

import jax
import jax.numpy as jnp
from jax import lax
from jax.sharding import PartitionSpec as P

HD = 64
G = 2048
K_SEL = 256
MOST = 128


EPS = 1e-05
NEG = -1e30


def rms_norm(values, gain):
    return values * lax.rsqrt(jnp.mean(values * values, axis=-1, keepdims=True) + EPS) * gain


def product(left, right):
    return jnp.dot(left, right, preferred_element_type=jnp.float32)


def contract_rows(left, right):
    return lax.dot_general(
        left, right, (((0,), (0,)), ((), ())), preferred_element_type=jnp.float32
    )


def contract_cols(left, right):
    return lax.dot_general(
        left, right, (((1,), (1,)), ((), ())), preferred_element_type=jnp.float32
    )


def split_heads(matrix):
    return matrix.reshape(matrix.shape[0], -1, HD)


def allowed_pairs(query_pos, query_seg, key_pos, key_seg):
    return (key_seg[None, :] == query_seg[:, None]) & (key_pos[None, :] <= query_pos[:, None])


def keep_state(old):
    return old


def unit_total(term):
    return lax.psum(term, "mlp")


def front(values, gain, weights):
    normed = rms_norm(values, gain).astype(jnp.bfloat16)
    query = product(normed, weights[0]).astype(jnp.bfloat16)
    keys = product(normed, weights[1]).astype(jnp.bfloat16)
    entries = product(normed, weights[2]).astype(jnp.bfloat16)
    return (normed, query, keys, entries)


def rest_forward(values, mixed_b, gain, projection, up_weight, down_weight):
    attn = unit_total(product(mixed_b, projection))
    hidden = values + attn
    normed = rms_norm(hidden, gain).astype(jnp.bfloat16)
    pre = product(normed, up_weight)
    active = jax.nn.gelu(pre).astype(jnp.bfloat16)
    mlp = unit_total(product(active, down_weight))
    return (attn, hidden, normed, pre, active, mlp)


def back_mlp(grad_mlp, hidden, normed, pre, active, gain, up_weight, down_weight):
    grad_down = contract_rows(active, grad_mlp)
    grad_active = contract_cols(grad_mlp, down_weight)
    gelu_pull = jax.vjp(jax.nn.gelu, pre)[1]
    grad_pre = gelu_pull(grad_active)[0].astype(jnp.bfloat16)
    grad_up = contract_rows(normed, grad_pre)
    grad_normed = unit_total(contract_cols(grad_pre, up_weight))
    norm_pull = jax.vjp(rms_norm, hidden, gain)[1]
    grad_hidden, grad_gain = norm_pull(grad_normed)
    return (grad_hidden, grad_gain, grad_up, grad_down)


def back_front(grad_query, grad_keys, grad_values, values, normed, gain, weights):
    grad_weights = jnp.stack(
        [
            contract_rows(normed, grad_query),
            contract_rows(normed, grad_keys),
            contract_rows(normed, grad_values),
        ]
    )
    partial_normed = (
        contract_cols(grad_query, weights[0])
        + contract_cols(grad_keys, weights[1])
        + contract_cols(grad_values, weights[2])
    )
    grad_normed = unit_total(partial_normed)
    norm_pull = jax.vjp(rms_norm, values, gain)[1]
    grad_values_in, grad_gain = norm_pull(grad_normed)
    return (grad_values_in, grad_gain, grad_weights)


def full_attention(query, keys, entries, query_pos, query_seg, key_pos, key_seg):
    scores = jnp.einsum("qhd,khd->hqk", query, keys, preferred_element_type=jnp.float32) * HD ** (
        -0.5
    )
    allowed = allowed_pairs(query_pos, query_seg, key_pos, key_seg)
    scores = jnp.where(allowed[None], scores, NEG)
    top = jnp.max(scores, axis=-1)
    weights = jnp.where(allowed[None], jnp.exp(scores - top[..., None]), 0.0)
    total = jnp.sum(weights, axis=-1)
    probs = (weights / total[..., None]).astype(jnp.bfloat16)
    mixed = jnp.einsum("hqk,khd->qhd", probs, entries, preferred_element_type=jnp.float32)
    return (mixed, top + jnp.log(total))


def pair_grads(
    query,
    grad_out,
    log_total,
    delta_rows,
    query_pos,
    query_seg,
    keys,
    entries,
    key_pos,
    key_seg,
    wanted,
):
    scale = HD ** (-0.5)
    scores = jnp.einsum("qhd,khd->hqk", query, keys, preferred_element_type=jnp.float32) * scale
    allowed = allowed_pairs(query_pos, query_seg, key_pos, key_seg)
    probs = jnp.where(allowed[None], jnp.exp(scores - log_total[..., None]), 0.0)
    grad_probs = jnp.einsum("qhd,khd->hqk", grad_out, entries, preferred_element_type=jnp.float32)
    grad_scores = (probs * (grad_probs - delta_rows[..., None])).astype(jnp.bfloat16)
    if wanted == "query":
        return (
            jnp.einsum("hqk,khd->qhd", grad_scores, keys, preferred_element_type=jnp.float32)
            * scale
        )
    grad_keys = (
        jnp.einsum("hqk,qhd->khd", grad_scores, query, preferred_element_type=jnp.float32) * scale
    )
    grad_entries = jnp.einsum(
        "hqk,qhd->khd", probs.astype(jnp.bfloat16), grad_out, preferred_element_type=jnp.float32
    )
    if wanted == "keys":
        return (grad_keys, grad_entries)
    grad_query = (
        jnp.einsum("hqk,khd->qhd", grad_scores, keys, preferred_element_type=jnp.float32) * scale
    )
    return (grad_query, grad_keys, grad_entries)


def blockwise(state, members, start, step):
    length = members[0].shape[0]
    width = math.gcd(length, 2048)

    def blockwise_one(carry, index):
        first = index * width
        part = tuple((lax.dynamic_slice_in_dim(member, first, width, 0) for member in members))
        return (step(carry, part, start + first), None)

    state, unused = lax.scan(blockwise_one, state, jnp.arange(length // width, dtype=jnp.int32))
    return state


def online_step(state, part, first_key, query, query_pos, query_seg):
    key_rows, value_rows, key_seg = part
    width = key_rows.shape[0]
    key_pos = first_key + jnp.arange(width, dtype=jnp.int32)

    def online_compute(old):
        top, total, acc = old
        scores = jnp.einsum(
            "qhd,khd->hqk", query, split_heads(key_rows), preferred_element_type=jnp.float32
        ) * HD ** (-0.5)
        allowed = allowed_pairs(query_pos, query_seg, key_pos, key_seg)
        scores = jnp.where(allowed[None], scores, NEG)
        new_top = jnp.maximum(top, jnp.max(scores, axis=-1))
        factor = jnp.exp(top - new_top)
        weights = jnp.where(allowed[None], jnp.exp(scores - new_top[..., None]), 0.0)
        total = total * factor + jnp.sum(weights, axis=-1)
        acc = acc * factor[..., None] + jnp.einsum(
            "hqk,khd->hqd",
            weights.astype(jnp.bfloat16),
            split_heads(value_rows),
            preferred_element_type=jnp.float32,
        )
        return (new_top, total, acc)

    return lax.cond(first_key <= query_pos[-1], online_compute, keep_state, state)


def query_step(grad, part, first_key, query, grad_out, log_total, delta_rows, query_pos, query_seg):
    key_rows, value_rows, key_seg = part
    key_pos = first_key + jnp.arange(key_rows.shape[0], dtype=jnp.int32)

    def query_compute(old):
        return old + pair_grads(
            query,
            grad_out,
            log_total,
            delta_rows,
            query_pos,
            query_seg,
            split_heads(key_rows),
            split_heads(value_rows),
            key_pos,
            key_seg,
            "query",
        )

    return lax.cond(first_key <= query_pos[-1], query_compute, keep_state, grad)


def body(inputs, segments, picks, gains, router, qkv, proj_out, up, down, cotangent):
    rows = inputs.shape[0]
    width = inputs.shape[1]
    ranks = lax.axis_size("seq")
    device = lax.axis_index("seq")
    local_width = qkv.shape[-1]
    heads = local_width // HD
    own = K_SEL * rows // G
    slots = MOST // ranks
    places = (picks + G * jnp.arange(picks.shape[0], dtype=jnp.int32)[:, None]).reshape(-1)
    picked_count = places.shape[0]
    holder = places // rows
    sources = jnp.arange(ranks, dtype=jnp.int32)
    lower = jnp.sum((holder[None, :] < sources[:, None]).astype(jnp.int32), axis=1)
    upper = jnp.sum((holder[None, :] <= sources[:, None]).astype(jnp.int32), axis=1)
    my_lower = lower[device]
    my_upper = upper[device]
    start_rank = my_lower + jnp.mod(sources - my_lower, ranks)
    slot_rank = start_rank[:, None] + ranks * jnp.arange(slots, dtype=jnp.int32)[None, :]
    filled = (slot_rank < my_upper).reshape(-1)
    slot_place = places[jnp.minimum(slot_rank, picked_count - 1)].reshape(-1)
    slot_row = jnp.where(filled, slot_place - device * rows, 0)
    outgoing = jnp.where(filled[:, None], inputs[slot_row], jnp.zeros((), jnp.bfloat16))
    outgoing_seg = jnp.where(filled, segments[slot_row], -1)
    arrived, arrived_seg = (
        lax.all_to_all(
            outgoing.reshape(ranks, slots, width), "seq", split_axis=0, concat_axis=0, tiled=True
        ),
        lax.all_to_all(
            outgoing_seg.reshape(ranks, slots), "seq", split_axis=0, concat_axis=0, tiled=True
        ),
    )
    mine = device + ranks * jnp.arange(own, dtype=jnp.int32)
    source = holder[mine]
    source_lower = lower[source]
    first_rank = source_lower + jnp.mod(device - source_lower, ranks)
    flat_index = source * slots + (mine - first_rank) // ranks
    picked = arrived.reshape(ranks * slots, width)[flat_index]
    picked_seg = arrived_seg.reshape(ranks * slots)[flat_index]
    picked_pos = places[mine]
    placing = (flat_index[:, None] == jnp.arange(ranks * slots, dtype=jnp.int32)[None, :]).astype(
        jnp.bfloat16
    )
    routed_rows = picked.astype(jnp.float32)
    normed_one, query_one, keys_one, values_one = front(routed_rows, gains[0, 0], qkv[0])
    key_all, value_all, pos_all, seg_all = (
        lax.all_gather(keys_one, "seq", axis=0, tiled=True),
        lax.all_gather(values_one, "seq", axis=0, tiled=True),
        lax.all_gather(picked_pos, "seq", axis=0, tiled=True),
        lax.all_gather(picked_seg, "seq", axis=0, tiled=True),
    )
    mixed_one, log_one = full_attention(
        split_heads(query_one),
        split_heads(key_all),
        split_heads(value_all),
        picked_pos,
        picked_seg,
        pos_all,
        seg_all,
    )
    mixed_one_b = mixed_one.reshape(own, local_width).astype(jnp.bfloat16)
    attn_one, hidden_one, normed_two_one, pre_one, active_one, mlp_one = rest_forward(
        routed_rows, mixed_one_b, gains[0, 1], proj_out[0], up[0], down[0]
    )
    change = (attn_one + mlp_one).astype(jnp.bfloat16)
    going_back = contract_rows(placing, change).astype(jnp.bfloat16)
    returned = lax.all_to_all(
        going_back.reshape(ranks, slots, width), "seq", split_axis=0, concat_axis=0, tiled=True
    )
    chosen = outgoing.astype(jnp.float32)
    gate = jax.nn.sigmoid(
        jnp.dot(chosen, router, precision=lax.Precision.HIGHEST, preferred_element_type=jnp.float32)
    )
    spread = (
        (slot_row[None, :] == jnp.arange(rows, dtype=jnp.int32)[:, None]) & filled[None, :]
    ).astype(jnp.float32)
    returned_f = returned.reshape(ranks * slots, width).astype(jnp.float32)
    first_out = inputs.astype(jnp.float32) + jnp.dot(
        spread,
        gate[:, None] * returned_f,
        precision=lax.Precision.HIGHEST,
        preferred_element_type=jnp.float32,
    )
    query_pos = device * rows + jnp.arange(rows, dtype=jnp.int32)
    normed_dense, query_dense, keys_dense, values_dense = front(first_out, gains[1, 0], qkv[1])
    query_heads = split_heads(query_dense)
    start_state = (
        jnp.full((heads, rows), NEG, jnp.float32),
        jnp.zeros((heads, rows), jnp.float32),
        jnp.zeros((heads, rows, HD), jnp.float32),
    )
    forward_part = partial(online_step, query=query_heads, query_pos=query_pos, query_seg=segments)
    top, total, acc = blockwise(
        start_state,
        (
            lax.all_gather(keys_dense, "seq", axis=0, tiled=True),
            lax.all_gather(values_dense, "seq", axis=0, tiled=True),
            lax.all_gather(segments, "seq", axis=0, tiled=True),
        ),
        jnp.int32(0),
        forward_part,
    )
    log_dense = top + jnp.log(total)
    mixed_heads = jnp.transpose(acc / total[..., None], (1, 0, 2))
    mixed_dense_b = mixed_heads.reshape(rows, local_width).astype(jnp.bfloat16)
    attn_dense, hidden_dense, normed_two_dense, pre_dense, active_dense, mlp_dense = rest_forward(
        first_out, mixed_dense_b, gains[1, 1], proj_out[1], up[1], down[1]
    )
    second_out = hidden_dense + mlp_dense
    grad_out = cotangent.astype(jnp.float32)
    grad_hidden_d, grad_gain_d2, grad_up_d, grad_down_d = back_mlp(
        cotangent,
        hidden_dense,
        normed_two_dense,
        pre_dense,
        active_dense,
        gains[1, 1],
        up[1],
        down[1],
    )
    grad_hidden_d = grad_out + grad_hidden_d
    grad_attn_d = grad_hidden_d.astype(jnp.bfloat16)
    grad_proj_d = contract_rows(mixed_dense_b, grad_attn_d)
    grad_mixed_d = contract_cols(grad_attn_d, proj_out[1]).astype(jnp.bfloat16)
    grad_heads = split_heads(grad_mixed_d)
    delta_dense = jnp.sum(grad_heads.astype(jnp.float32) * mixed_heads, axis=-1).T
    query_part = partial(
        query_step,
        query=query_heads,
        grad_out=grad_heads,
        log_total=log_dense,
        delta_rows=delta_dense,
        query_pos=query_pos,
        query_seg=segments,
    )
    zero_heads = jnp.zeros((rows, heads, HD), jnp.float32)
    key_every, value_every, seg_every = (
        lax.all_gather(keys_dense, "seq", axis=0, tiled=True),
        lax.all_gather(values_dense, "seq", axis=0, tiled=True),
        lax.all_gather(segments, "seq", axis=0, tiled=True),
    )
    grad_query_d = blockwise(zero_heads, (key_every, value_every, seg_every), 0, query_part)
    step_width = math.gcd(rows * lax.axis_size("seq"), 2048)

    def key_one(index):
        first = index * step_width
        keys_part = lax.dynamic_slice_in_dim(key_every, first, step_width, 0)
        values_part = lax.dynamic_slice_in_dim(value_every, first, step_width, 0)
        seg_part = lax.dynamic_slice_in_dim(seg_every, first, step_width, 0)
        key_pos = first + jnp.arange(step_width, dtype=jnp.int32)

        def key_compute(unused):
            grad_keys, grad_entries = pair_grads(
                query_heads,
                grad_heads,
                log_dense,
                delta_dense,
                query_pos,
                segments,
                split_heads(keys_part),
                split_heads(values_part),
                key_pos,
                seg_part,
                "keys",
            )
            return jnp.stack(
                [
                    grad_keys.reshape(step_width, local_width),
                    grad_entries.reshape(step_width, local_width),
                ],
                axis=1,
            )

        def empty(unused):
            return jnp.zeros((step_width, 2, local_width), jnp.float32)

        return lax.cond(first <= query_pos[-1], key_compute, empty, 0)

    pieces = lax.map(
        key_one, jnp.arange(rows * lax.axis_size("seq") // step_width, dtype=jnp.int32)
    )
    terms = lax.psum_scatter(
        pieces.reshape(rows * lax.axis_size("seq"), 2, local_width),
        "seq",
        scatter_dimension=0,
        tiled=True,
    )
    grad_keys_d = terms[:, 0]
    grad_values_d = terms[:, 1]
    grad_query_b = grad_query_d.reshape(rows, local_width).astype(jnp.bfloat16)
    grad_first_norm, grad_gain_d1, grad_qkv_d = back_front(
        grad_query_b,
        grad_keys_d.astype(jnp.bfloat16),
        grad_values_d.astype(jnp.bfloat16),
        first_out,
        normed_dense,
        gains[1, 0],
        qkv[1],
    )
    grad_first = grad_hidden_d + grad_first_norm
    grad_slot = jnp.where(filled[:, None], grad_first[slot_row], 0.0)
    grad_gate = jnp.sum(grad_slot * returned_f, axis=-1)
    grad_logit = jnp.where(filled, grad_gate * gate * (1.0 - gate), 0.0)
    grad_router = jnp.dot(
        grad_logit, chosen, precision=lax.Precision.HIGHEST, preferred_element_type=jnp.float32
    )
    sent_grad = (gate[:, None] * grad_slot).astype(jnp.bfloat16)
    arrived_grad = lax.all_to_all(
        sent_grad.reshape(ranks, slots, width), "seq", split_axis=0, concat_axis=0, tiled=True
    )
    grad_change = arrived_grad.reshape(ranks * slots, width)[flat_index]
    grad_hidden_r, grad_gain_r2, grad_up_r, grad_down_r = back_mlp(
        grad_change, hidden_one, normed_two_one, pre_one, active_one, gains[0, 1], up[0], down[0]
    )
    grad_attn_r = (grad_change.astype(jnp.float32) + grad_hidden_r).astype(jnp.bfloat16)
    grad_proj_r = contract_rows(mixed_one_b, grad_attn_r)
    grad_mixed_r = contract_cols(grad_attn_r, proj_out[0]).astype(jnp.bfloat16)
    grad_heads_r = split_heads(grad_mixed_r)
    delta_routed = jnp.sum(grad_heads_r.astype(jnp.float32) * mixed_one, axis=-1).T
    grad_query_r, grad_keys_all, grad_values_all = pair_grads(
        split_heads(query_one),
        grad_heads_r,
        log_one,
        delta_routed,
        picked_pos,
        picked_seg,
        split_heads(key_all),
        split_heads(value_all),
        pos_all,
        seg_all,
        "both",
    )
    routed_terms = jnp.stack(
        [
            grad_keys_all.reshape(picked_count, local_width),
            grad_values_all.reshape(picked_count, local_width),
        ],
        axis=1,
    )
    routed_share = lax.psum_scatter(routed_terms, "seq", scatter_dimension=0, tiled=True)
    grad_rows_norm, grad_gain_r1, grad_qkv_r = back_front(
        grad_query_r.reshape(own, local_width).astype(jnp.bfloat16),
        routed_share[:, 0].astype(jnp.bfloat16),
        routed_share[:, 1].astype(jnp.bfloat16),
        routed_rows,
        normed_one,
        gains[0, 0],
        qkv[0],
    )
    grad_rows = (grad_hidden_r + grad_rows_norm).astype(jnp.bfloat16)
    back_slots = contract_rows(placing, grad_rows).astype(jnp.bfloat16)
    arrived_back = lax.all_to_all(
        back_slots.reshape(ranks, slots, width), "seq", split_axis=0, concat_axis=0, tiled=True
    )
    slot_grad = (
        arrived_back.reshape(ranks * slots, width).astype(jnp.float32)
        + grad_logit[:, None] * router[None, :]
    )
    grad_input = grad_first + jnp.dot(
        spread, slot_grad, precision=lax.Precision.HIGHEST, preferred_element_type=jnp.float32
    )
    gain_grads = jnp.stack(
        [jnp.stack([grad_gain_r1, grad_gain_r2]), jnp.stack([grad_gain_d1, grad_gain_d2])]
    )
    summed = (
        lax.psum_scatter(gain_grads, "seq", scatter_dimension=2, tiled=True),
        lax.psum_scatter(grad_router, "seq", scatter_dimension=0, tiled=True),
        lax.psum_scatter(
            jnp.stack([grad_qkv_r, grad_qkv_d]), "seq", scatter_dimension=2, tiled=True
        ),
        lax.psum_scatter(
            jnp.stack([grad_proj_r, grad_proj_d]), "seq", scatter_dimension=2, tiled=True
        ),
        lax.psum_scatter(jnp.stack([grad_up_r, grad_up_d]), "seq", scatter_dimension=1, tiled=True),
        lax.psum_scatter(
            jnp.stack([grad_down_r, grad_down_d]), "seq", scatter_dimension=2, tiled=True
        ),
    )
    return (
        first_out.astype(jnp.bfloat16),
        second_out.astype(jnp.bfloat16),
        grad_input,
        summed[0],
        summed[1],
        summed[2],
        summed[3],
        summed[4],
        summed[5],
    )


def solution(mesh):
    placed = (
        P("seq", None),
        P("seq"),
        P(),
        P(),
        P(),
        P(None, None, None, "mlp"),
        P(None, "mlp", None),
        P(None, None, "mlp"),
        P(None, "mlp", None),
        P("seq", None),
    )
    return jax.shard_map(
        body,
        mesh=mesh,
        in_specs=placed,
        out_specs=(
            P("seq", None),
            P("seq", None),
            P("seq", None),
            P(None, None, "seq"),
            P("seq"),
            P(None, None, "seq", "mlp"),
            P(None, "mlp", "seq"),
            P(None, "seq", "mlp"),
            P(None, "mlp", "seq"),
        ),
        check_vma=False,
    )
```

profile of v0, /device:TPU:0, one launch (start us, length us, event | category | flops | bytes accessed | tf_op | source)
XLA Modules:
  0.0 1068.9 jit_solution(3205969325469289675)
XLA Ops:
  15.8 7.4 all-to-all-start.1
  38.1 12.3 %all-reduce.6 = (s32[256]{0:T(256)S(1)}, s32[256]{0:T(256)S(1)}) all-reduce(s32[256]{0:T(256)S(1)} %dynamic-update-slice.1, s32[256]{0:T(256)S(1)} %dynamic-update-slice), channel_id=3, replica_groups=mesh['seq'=16,'mlp'=2] {'seq'}, use_global_device_ids=true, to_apply=%add.1 | all-reduce | flops 512 | bytes 4096
  55.2 18.5 %all_gather.27 = bf16[256,384]{1,0:T(8,128)(2,1)S(1)} all-gather(bf16[16,384]{1,0:T(8,128)(2,1)S(1)} %convolution_convert_fusion.7), channel_id=1, replica_groups=mesh['seq'=16,'mlp'=2] {'seq'}, dimensions={0}, use_global_device_ids=true | all-gather | bytes 208896 | tf_op jit(solution)/shard_map/all_gather | solution.py:264
  73.9 18.8 %all_gather.24 = bf16[256,384]{1,0:T(8,128)(2,1)S(1)} all-gather(bf16[16,384]{1,0:T(8,128)(2,1)S(1)} %convolution_convert_fusion.9), channel_id=1, replica_groups=mesh['seq'=16,'mlp'=2] {'seq'}, dimensions={0}, use_global_device_ids=true | all-gather | bytes 208896 | tf_op jit(solution)/shard_map/all_gather | solution.py:265
  94.5 8.6 psum.56
  107.6 7.7 psum.57
  120.3 8.5 all-to-all-done.2
  136.8 18.2 %all-gather.2 = s32[16,1,128]{2,1,0:T(1,128)S(1)} all-gather(s32[1,1,128]{2,1,0:T(1,128)S(1)} %bitcast.273), channel_id=1, replica_groups=mesh['seq'=16,'mlp'=2] {'seq'}, dimensions={0}, use_global_device_ids=true | all-gather | bytes 8704 | tf_op jit(solution)/shard_map/all_gather | solution.py:315
  157.1 12.2 %all-gather.6.cloned.1.call-done = bf16[2048,384]{1,0:T(8,128)(2,1)} async-done(((bf16[128,384]{1,0:T(8,128)(2,1)}), bf16[2048,384]{1,0:T(8,128)(2,1)}) %all-gather.6.cloned.1.call-update) | async-done | bytes 1572880 | tf_op jit(solution)/shard_map/all_gather | solution.py:313
  169.4 41.4 %all-gather.8.cloned.1.call-done = bf16[2048,384]{1,0:T(8,128)(2,1)} async-done(((bf16[128,384]{1,0:T(8,128)(2,1)}), bf16[2048,384]{1,0:T(8,128)(2,1)}) %all-gather.8.cloned.1.call-update) | async-done | bytes 1572880 | tf_op jit(solution)/shard_map/all_gather | solution.py:314
  210.8 17.2 %conditional.3 = (f32[6,128]{1,0:T(8,128)S(1)}, f32[6,128,64]{1,2,0:T(8,128)}, f32[6,128]{1,0:T(8,128)S(1)}) conditional(s32[]{:T(128)} %bitcast.35, (f32[6,128]{1,0:T(8,128)S(1)}, f32[6,128]{1,0:T(8,128)S(1)}, f32[6,128,64]{1,2,0:T(8,128)}) %tuple.44, (s32[2048]{0:T(1024)S(1)}, s32[128]{0:T(128)S(1)}, s32[2048]{0:T(1024)S(1)}, ...), branch_computations={%region_9.10_spmd.clone, %region_10.13_spmd.clone} | conditional | flops 423987456 | bytes 61372496 | solution.py:193
  222.1 5.9 fusion.23
  230.8 24.7 %all-reduce.16.cloned.1.call-done = f32[128,768]{1,0:T(8,128)} async-done(((f32[128,768]{1,0:T(8,128)}), f32[128,768]{1,0:T(8,128)}) %all-reduce.16.cloned.1.call-update) | async-done | bytes 393232 | tf_op jit(solution)/shard_map/psum | solution.py:52
  266.2 25.8 %all-reduce.18.cloned.1.call-done = f32[128,768]{1,0:T(8,128)} async-done(((f32[128,768]{1,0:T(8,128)}), f32[128,768]{1,0:T(8,128)}) %all-reduce.18.cloned.1.call-update) | async-done | bytes 393232 | tf_op jit(solution)/shard_map/psum | solution.py:52
  302.3 25.9 %conditional.5 = (f32[2048,2,384]{0,2,1:T(8,128)}) conditional(s32[]{:T(128)} %bitcast.35, () %tuple.47, (s32[2048]{0:T(1024)S(1)}, s32[128]{0:T(128)S(1)}, s32[2048]{0:T(1024)}, s32[128]{0:T(128)}, bf16[2048,384]{1,0:T(8,128)(2,1)S(1)}, /*index=5*/bf16[128,6,64]{0,2,1:T(8,128)(2,1)}, f32[6,128]{1,0:T(8,128)}, bf16[2048,384]{1,0:T(8,128)(2,1)S(1)}, ...), branch_computations={%region_21.22_spmd, %region_22.23_spmd} | conditional | flops 824180736 | bytes 61007936 | solution.py:394
  304.2 5.2 fusion.213
  312.7 7.9 convolution_multiply_fusion
  332.8 17.9 %conditional.4 = (f32[128,6,64]{0,2,1:T(8,128)}) conditional(s32[]{:T(128)} %bitcast.35, f32[128,6,64]{0,2,1:T(8,128)} %broadcast_in_dim.211, (s32[2048]{0:T(1024)S(1)}, s32[128]{0:T(128)S(1)}, s32[2048]{0:T(1024)}, s32[128]{0:T(128)}, bf16[2048,384]{1,0:T(8,128)(2,1)S(1)}, /*index=5*/bf16[128,6,64]{0,2,1:T(8,128)(2,1)}, f32[6,128]{1,0:T(8,128)}, ...), branch_computations={%region_19.20_spmd, %region_20.21_spmd} | conditional | flops 614301696 | bytes 31022116 | solution.py:215
  334.4 5.4 fusion.212
  342.5 7.8 fusion.3
  353.2 60.4 %reduce-scatter.7.cloned.1.call-done = f32[128,2,384]{0,2,1:T(8,128)} async-done(((f32[2048,2,384]{0,2,1:T(8,128)}), f32[128,2,384]{0,2,1:T(8,128)}) %reduce-scatter.7.cloned.1.call-update) | async-done | bytes 393232 | tf_op jit(solution)/shard_map/reduce_scatter | solution.py:399
  421.4 29.9 %all-reduce.22.cloned.1.call-done = (f32[128,768]{1,0:T(8,128)}, f32[128,768]{1,0:T(8,128)}) async-done(((f32[128,768]{1,0:T(8,128)}, f32[128,768]{1,0:T(8,128)}), (f32[128,768]{1,0:T(8,128)}, f32[128,768]{1,0:T(8,128)})) %all-reduce.22.cloned.1.call-update) | async-done | bytes 786448 | tf_op jit(solution)/shard_map/psum | solution.py:52
  456.3 5.6 all-to-all-start.3
  463.7 7.2 all-to-all-done.3
  479.7 7.7 psum.62
  493.5 67.1 %all-reduce.23 = (bf16[256,2,384]{2,1,0:T(2,128)(2,1)S(1)}, f32[768]{0:T(1024)}) all-reduce(f32[256,2,384]{2,1,0:T(2,128)S(1)} %pad_maximum_fusion.5, f32[768]{0:T(1024)S(1)} %convolution_reduce_fusion), channel_id=5, replica_groups=mesh['seq'=16,'mlp'=2] {'seq'}, use_global_device_ids=true, to_apply=%region_29.30.clone | all-reduce | flops 197376 | bytes 1185792
  563.3 8.6 psum.63
  574.4 8.2 pad_maximum_fusion.2
  582.8 15.0 %copy.130 = f32[2,1536,768]{1,0,2:T(2,128)} copy(f32[2,1536,768]{2,1,0:T(8,128)} %pad_maximum_fusion.2) | data formatting | bytes 18874368 | tf_op jit(solution)/shard_map/stack | solution.py:493
  633.3 217.8 %all-reduce.20.cloned.1.call-done = (f32[2,384,768]{1,0,2:T(2,128)}, f32[2,1536,768]{1,0,2:T(2,128)}) async-done(((f32[2,384,768]{1,0,2:T(2,128)}, f32[2,1536,768]{1,0,2:T(2,128)}), (f32[2,384,768]{1,0,2:T(2,128)}, f32[2,1536,768]{1,0,2:T(2,128)})) %all-reduce.20.cloned.1.call-update) | async-done | bytes 11796496
  854.8 91.7 %reduce-scatter.9.cloned.1.call-done = f32[2,3,48,384]{3,2,1,0:T(8,128)} async-done(((f32[2,3,768,384]{3,2,1,0:T(8,128)}), f32[2,3,48,384]{3,2,1,0:T(8,128)}) %reduce-scatter.9.cloned.1.call-update) | async-done | bytes 442384 | tf_op jit(solution)/shard_map/reduce_scatter | solution.py:485
  946.4 115.4 %reduce-scatter.11.cloned.1.call-done = f32[2,48,1536]{2,1,0:T(8,128)} async-done(((f32[2,768,1536]{2,1,0:T(8,128)}), f32[2,48,1536]{2,1,0:T(8,128)}) %reduce-scatter.11.cloned.1.call-update) | async-done | bytes 589840 | tf_op jit(solution)/shard_map/reduce_scatter | solution.py:491
  (433 shorter events, 178.3 us)
Async XLA Ops:
  10.8 118.0 %copy-start.78 = (pred[128]{0:T(512)(128)(4,1)}, pred[128]{0:T(512)(128)(4,1)S(1)}, u32[]{:S(2)}) copy-start(pred[128]{0:T(512)(128)(4,1)S(1)} %lt.156) | copy-start | bytes 388
  12.3 116.6 %copy-start.91 = (s32[128]{0:T(128)}, s32[128]{0:T(128)S(1)}, u32[]{:S(2)}) copy-start(s32[128]{0:T(128)S(1)} %get-tuple-element.484) | copy-start | bytes 1540
  15.8 13.7 %all-to-all-start.1 = ((s32[16,1,8]{2,1,0:T(1,128)}), s32[16,1,8]{2,1,0:T(1,128)S(1)}, u32[]{:S(2)}, u32[]{:S(2)}) async-start(s32[16,1,8]{2,1,0:T(1,128)} %bitcast.24), calls=%async_computation.1 | async-start | bytes 16384 | tf_op jit(solution)/shard_map/all_to_all | solution.py:246
  24.2 95.8 %copy-start.39 = (bf16[128,768]{1,0:T(8,128)(2,1)}, bf16[128,768]{1,0:T(8,128)(2,1)S(1)}, u32[]{:S(2)}) copy-start(bf16[128,768]{1,0:T(8,128)(2,1)S(1)} %gather_fusion.1) | copy-start | bytes 589828
  24.9 69.4 %copy-start.12 = (bf16[2,384,768]{2,1,0:T(8,128)(2,1)S(1)}, bf16[2,384,768]{2,1,0:T(8,128)(2,1)}, u32[]{:S(2)}) copy-start(bf16[2,384,768]{2,1,0:T(8,128)(2,1)} %param.22) | copy-start | bytes 3538948
  26.3 88.9 %copy-start.93 = (s32[16]{0:T(128)}, s32[16]{0:T(128)S(1)}, u32[]{:S(2)}) copy-start(s32[16]{0:T(128)S(1)} %fusion.194) | copy-start | bytes 196
  29.6 21.0 %all-to-all-start = ((bf16[16,8,768]{2,1,0:T(8,128)(2,1)}), bf16[16,8,768]{2,1,0:T(8,128)(2,1)S(1)}, u32[]{:S(2)}, u32[]{:S(2)}) async-start(bf16[16,8,768]{2,1,0:T(8,128)(2,1)} %bitcast_select_fusion.1), calls=%async_computation | async-start | bytes 393216 | tf_op jit(solution)/shard_map/all_to_all | solution.py:243
  35.9 69.5 %copy-start.58 = (f32[768]{0:T(1024)}, f32[768]{0:T(1024)S(1)}, u32[]{:S(2)}) copy-start(f32[768]{0:T(1024)S(1)} %get-tuple-element.466) | copy-start | bytes 9220
  35.9 93.5 %copy-start.64 = (f32[768]{0:T(1024)}, f32[768]{0:T(1024)S(1)}, u32[]{:S(2)}) copy-start(f32[768]{0:T(1024)S(1)} %get-tuple-element.468) | copy-start | bytes 9220
  116.3 12.5 %all-to-all-start.2 = ((bf16[16,8,768]{2,1,0:T(8,128)(2,1)}), bf16[16,8,768]{2,1,0:T(8,128)(2,1)S(1)}, u32[]{:S(2)}, u32[]{:S(2)}) async-start(bf16[16,8,768]{2,1,0:T(8,128)(2,1)} %fusion.53), calls=%async_computation.2 | async-start | bytes 393216 | tf_op jit(solution)/shard_map/all_to_all | solution.py:284
  119.8 49.5 %all-gather.6.cloned.1.call-start = ((), (), s32[]{:S(2)}) async-start(), calls=%async_computation.9 | async-start | bytes 1671168 | tf_op jit(solution)/shard_map/all_gather | solution.py:313
  120.3 90.5 %copy-start.95 = (f32[128]{0:T(128)}, f32[128]{0:T(128)S(1)}, u32[]{:S(2)}) copy-start(f32[128]{0:T(128)S(1)} %fusion.62) | copy-start | bytes 1540
  128.8 82.0 %copy-start.23 = (bf16[16,8,768]{2,1,0:T(8,128)(2,1)}, bf16[16,8,768]{2,1,0:T(8,128)(2,1)S(1)}, u32[]{:S(2)}) copy-start(bf16[16,8,768]{2,1,0:T(8,128)(2,1)S(1)} %all-to-all-done.2) | copy-start | bytes 589828
  129.3 81.5 %copy-start.104 = (f32[128]{0:T(128)}, f32[128]{0:T(128)S(1)}, u32[]{:S(2)}) copy-start(f32[128]{0:T(128)S(1)} %get-tuple-element.502) | copy-start | bytes 1540
  129.4 126.1 %copy-start.7 = (f32[128,768]{1,0:T(8,128)}, f32[128,768]{1,0:T(8,128)S(1)}, u32[]{:S(2)}) copy-start(f32[128,768]{1,0:T(8,128)S(1)} %get-tuple-element.503) | copy-start | bytes 1179652
  129.4 81.4 %copy-start.97 = (f32[128]{0:T(128)}, f32[128]{0:T(128)S(1)}, u32[]{:S(2)}) copy-start(f32[128]{0:T(128)S(1)} %fusion.197) | copy-start | bytes 1540
  129.5 81.3 %copy-start.16 = (bf16[128,768]{1,0:T(8,128)(2,1)}, bf16[128,768]{1,0:T(8,128)(2,1)S(1)}, u32[]{:S(2)}) copy-start(bf16[128,768]{1,0:T(8,128)(2,1)S(1)} %multiply_convert_fusion.5) | copy-start | bytes 589828
  131.6 79.2 %all-gather.8.cloned.1.call-start = ((), (), s32[]{:S(2)}) async-start(), calls=%async_computation.10 | async-start | bytes 1671168 | tf_op jit(solution)/shard_map/all_gather | solution.py:314
  133.7 121.8 %all-reduce.16.cloned.1.call-start = ((), (), s32[]{:S(2)}) async-start(), calls=%async_computation.11 | async-start | bytes 786432 | tf_op jit(solution)/shard_map/psum | solution.py:52
  230.7 61.3 %all-reduce.18.cloned.1.call-start = ((), (), s32[]{:S(2)}) async-start(), calls=%async_computation.12 | async-start | bytes 786432 | tf_op jit(solution)/shard_map/psum | solution.py:52
  266.2 147.4 %reduce-scatter.7.cloned.1.call-start = ((), (), s32[]{:S(2)}) async-start(), calls=%async_computation.13 | async-start | bytes 6684672 | tf_op jit(solution)/shard_map/reduce_scatter | solution.py:399
  328.2 123.0 %all-reduce.22.cloned.1.call-start = ((), (), s32[]{:S(2)}) async-start(), calls=%async_computation.18 | async-start | bytes 1572864 | tf_op jit(solution)/shard_map/psum | solution.py:52
  350.7 67.6 %copy-start.20 = (f32[128,1536]{1,0:T(8,128)S(1)}, f32[128,1536]{1,0:T(8,128)}, u32[]{:S(2)}) copy-start(f32[128,1536]{1,0:T(8,128)} %copy-done.19) | copy-start | bytes 2359300
  350.7 67.6 %copy-start.34 = (bf16[128,768]{1,0:T(8,128)(2,1)S(1)}, bf16[128,768]{1,0:T(8,128)(2,1)}, u32[]{:S(2)}) copy-start(bf16[128,768]{1,0:T(8,128)(2,1)} %param.25) | copy-start | bytes 589828
  456.3 14.6 %all-to-all-start.3 = ((bf16[16,8,768]{2,1,0:T(8,128)(2,1)}), bf16[16,8,768]{2,1,0:T(8,128)(2,1)S(1)}, u32[]{:S(2)}, u32[]{:S(2)}) async-start(bf16[16,8,768]{2,1,0:T(8,128)(2,1)} %get-tuple-element.491), calls=%async_computation.4 | async-start | bytes 393216 | tf_op jit(solution)/shard_map/all_to_all | solution.py:425
  461.9 164.6 %reduce-scatter.13.cloned.1.call-start = ((), (), s32[]{:S(2)}) async-start(), calls=%async_computation.16 | async-start | bytes 417792
  490.0 81.9 %copy-start.28 = (bf16[16,768]{1,0:T(8,128)(2,1)S(1)}, bf16[16,768]{1,0:T(8,128)(2,1)}, u32[]{:S(2)}) copy-start(bf16[16,768]{1,0:T(8,128)(2,1)} %copy-done.27) | copy-start | bytes 73732
  490.0 81.9 %copy-start.81 = (f32[16]{0:T(128)S(1)}, f32[16]{0:T(128)}, u32[]{:S(2)}) copy-start(f32[16]{0:T(128)} %copy-done.80) | copy-start | bytes 196
  574.4 276.7 %all-reduce.20.cloned.1.call-start = ((), (), s32[]{:S(2)}) async-start(), calls=%async_computation.17 | async-start | bytes 23592960
  600.9 345.6 %reduce-scatter.9.cloned.1.call-start = ((), (), s32[]{:S(2)}) async-start(), calls=%async_computation.14 | async-start | bytes 7520256 | tf_op jit(solution)/shard_map/reduce_scatter | solution.py:485
  610.5 451.3 %reduce-scatter.11.cloned.1.call-start = ((), (), s32[]{:S(2)}) async-start(), calls=%async_computation.15 | async-start | bytes 10027008 | tf_op jit(solution)/shard_map/reduce_scatter | solution.py:491
  619.6 12.5 %all-to-all-start.4 = ((bf16[16,8,768]{2,1,0:T(8,128)(2,1)}), bf16[16,8,768]{2,1,0:T(8,128)(2,1)S(1)}, u32[]{:S(2)}, u32[]{:S(2)}) async-start(bf16[16,8,768]{2,1,0:T(8,128)(2,1)} %fusion.54), calls=%async_computation.5 | async-start | bytes 393216 | tf_op jit(solution)/shard_map/all_to_all | solution.py:469
  (93 other events, 1463.0 us)
Sparse Core Ops, SparseCore 0:
  131.7 37.5 all-gather.5
  172.2 38.5 all-gather.7
  230.9 24.5 all-reduce.15
  266.3 25.7 all-reduce.17
  328.3 85.2 reduce-scatter.6
  417.5 33.6 all-reduce.21
  574.5 51.9 reduce-scatter.12
  630.8 220.2 all-reduce.19
  856.2 90.1 reduce-scatter.8
  951.0 110.8 reduce-scatter.10
where the time goes:
time: 1080 us; the launch traced here: 1070 us
  waiting for transfers between devices  643 us (60%)
  blocking collectives  168 us (16%)
  matrix products  103 us (10%)
  local copies, waits for them, and re-layouts  64.5 us (6%)
  other arithmetic  47 us (4%)
  starting transfers between devices  24.2 us (2%)
  between operations  18.7 us (2%)
    unnamed x12, waiting for transfers between devices  219 us
    reduce_scatter x1, waiting for transfers between devices, body(): lax.psum_scatter(jnp.stack([grad_up_r, grad_up_d]), 'seq', scatter_dimens...  115 us
    reduce_scatter x1, waiting for transfers between devices, body(): lax.psum_scatter(jnp.stack([grad_qkv_r, grad_qkv_d]), 'seq', scatter_dime...  91.7 us
    psum x3, waiting for transfers between devices, unit_total(): return lax.psum(term, 'mlp')  80.4 us
    unnamed x2, blocking collectives  79.4 us
    reduce_scatter x1, waiting for transfers between devices, body(): lax.psum_scatter(pieces.reshape(rows * lax.axis_size('seq'), 2, local_wid...  60.4 us
    all_gather x1, waiting for transfers between devices, body(): lax.all_gather(values_dense, 'seq', axis=0, tiled=True)  41.4 us
    psum x4, blocking collectives, unit_total(): return lax.psum(term, 'mlp')  32.6 us
  transfers between devices with their start and end apart: 15, of which 14 were waited for; matrix products, arithmetic and copies ran while one was open for 9% of the time, Pallas kernels for 0%

commit v1 on v0

v1 whole, which is shorter than its diff:
```python
from types import SimpleNamespace

import jax
import jax.numpy as jnp
import numpy as np
from jax import lax
from jax.experimental import pallas as pl
from jax.experimental.pallas import tpu as pltpu
from jax.sharding import PartitionSpec as P

HD = 64
G = 2048
EPS = 1e-05
NEG = -1e30
SCALE = HD**-0.5
BF = jnp.bfloat16
F32 = jnp.float32
MESH = pl.DeviceIdType.MESH
DMA = pltpu.SemaphoreType.DMA
GELU_A = 0.044715
GELU_B = float(np.sqrt(2.0 / np.pi))
KINDS = ("down", "up", "proj", "qkv")


def dot(left, right, dims):
    return lax.dot_general(left, right, (dims, ((), ())), preferred_element_type=F32)


def nn(left, right):
    return dot(left, right, ((1,), (0,)))


def nt(left, right):
    return dot(left, right, ((1,), (1,)))


def tn(left, right):
    return dot(left, right, ((0,), (0,)))


def inverse_rms(x):
    return lax.rsqrt(jnp.mean(x * x, axis=-1, keepdims=True) + EPS)


def rms(x, gain):
    return x * inverse_rms(x) * gain


def rms_back(dy, x, gain):
    r = inverse_rms(x)
    gy = gain * dy
    dx = r * gy - x * (r * r * r) * jnp.mean(gy * x, axis=-1, keepdims=True)
    return dx, jnp.sum(dy * x * r, axis=0, keepdims=True)


def gelu_pair(x):
    t = jnp.tanh(GELU_B * (x + GELU_A * x * x * x))
    half = 0.5 * (1.0 + t)
    slope = half + 0.5 * x * (1.0 - t * t) * (GELU_B * (1.0 + 3.0 * GELU_A * x * x))
    return x * half, slope


def column(row):
    wide = jnp.broadcast_to(row.astype(F32), (128, row.shape[1]))
    return jnp.transpose(wide)[:, 0:1]


def chunks(extent):
    width = 384 if extent % 384 == 0 else extent
    return [(at, width) for at in range(0, extent, width)]


def build(S, n, T, D, W, F, R, groups):
    rest = S // 2
    Y = 2 ** ((rest.bit_length() - 1) // 2)
    Z = rest // Y
    ZY = Z * Y
    H = W // HD
    LEVEL = 2 * Y
    CH = LEVEL * T
    GN = R // T
    RH = R // GN
    RB = R // S
    DM = D // n
    DR = D // S
    DRP = -(-DR // 16) * 16
    Q = ZY * DRP
    XW = {"down": F, "up": F, "proj": W, "qkv": 3 * W}

    target = np.full((2, 1, Q), -1, np.int32)
    for core in range(2):
        for yy in range(Y):
            for zz in range(Z):
                for j in range(DR):
                    target[core, 0, (yy * Z + zz) * DRP + j] = ((zz * Y + yy) * 2 + core) * DR + j

    ins = ["inp", "segr", "picks", "gains", "router", "cot", "target", "qkv_h", "proj_h", "up_h", "down_h"]
    outs = {
        "ro_o": ((T, D), BF),
        "do_o": ((T, D), BF),
        "gi_o": ((T, D), F32),
        "sm_o": ((8, 128), F32),
        "rg_o": ((2, D), F32),
        "qkv_o": ((2, 3, DR, W), F32),
        "proj_o": ((2, W, DR), F32),
        "up_o": ((2, DR, F), F32),
        "down_o": ((2, F, DR), F32),
    }
    vm = {
        "wq": ((2, 3, D, W), BF),
        "wp": ((2, W, D), BF),
        "wu": ((2, D, F), BF),
        "wd": ((2, F, D), BF),
        "sega": ((S, 8, T), jnp.int32),
        "segc": ((T, 1), F32),
        "oht": ((T, R), BF),
        "oh": ((R, T), BF),
        "posr": ((GN, 8, RH), F32),
        "posc": ((RH, 1), F32),
        "sgr": ((GN, 8, RH), F32),
        "sgc": ((RH, 1), F32),
        "part": ((S, RB, DM), BF),
        "r1": ((S, RB, DM), BF),
        "full": ((2, n * ZY, RB, DM), BF),
        "rows": ((R, D), BF),
        "nr": ((RH, D), BF),
        "chh": ((RH, D), BF),
        "qr": ((R, W), BF),
        "kr": ((R, W), BF),
        "vr": ((R, W), BF),
        "mr": ((H, RH, 1), F32),
        "lr": ((H, RH, 1), F32),
        "ar": ((H, RH, HD), F32),
        "mixr": ((RH, W), BF),
        "attr": ((RH, D), F32),
        "n2r": ((RH, D), BF),
        "prer": ((RH, F), F32),
        "actr": ((RH, F), BF),
        "xr": ((2, n, RH, D), BF),
        "xd": ((3, n, T, D), BF),
        "chg": ((GN, RH, D), BF),
        "sel": ((T, D), BF),
        "ro": ((T, D), F32),
        "nd": ((T, D), BF),
        "kva": ((S, T, 2 * W), BF),
        "qa": ((S, T, W), BF),
        "da": ((S, T, W), BF),
        "sta": ((S, 16, T), F32),
        "md": ((H, T, 1), F32),
        "ld": ((H, T, 1), F32),
        "ad": ((H, T, HD), F32),
        "mixd": ((T, W), BF),
        "hid": ((T, D), F32),
        "n2d": ((T, D), BF),
        "dact": ((T, F), F32),
        "actd": ((T, F), BF),
        "dpre": ((T, F), BF),
        "dattn": ((T, D), BF),
        "dq": ((H, max(T, RH), HD), F32),
        "dk": ((H, max(T, RH), HD), F32),
        "dv": ((H, max(T, RH), HD), F32),
        "g3": ((T, 3 * W), BF),
        "dro": ((T, D), F32),
        "small": ((8, D), F32),
        "sblk": ((S, 8, 128), F32),
        "srec": ((S, 8, 128), F32),
        "dor": ((GN, RH, W), BF),
        "str": ((GN, 16, RH), F32),
        "dprer": ((RH, F), BF),
        "dattr": ((RH, D), BF),
        "g3r": ((RH, 3 * W), BF),
        "gr": ((GN, 8, D), F32),
        "sele": ((2, D, Q), BF),
    }
    for k in KINDS:
        X = XW[k]
        vm["keep_" + k] = ((Y, Z, DRP, X), F32)
        vm["send_" + k] = ((Y, Z, DRP, X), BF)
        vm["sibr_" + k] = ((Y, Z, DRP, X), BF)
        vm["yrec_" + k] = ((Y - 1, Z, DRP, X), BF)
        vm["zrec_" + k] = ((Z - 1, DRP, X), BF)
        vm["rsend_" + k] = ((GN - 1, DRP, X), BF)
        vm["rkeep_" + k] = ((DRP, X), F32)
        vm["rrec_" + k] = ((GN - 1, DRP, X), BF)
    n_sends = (Z - 1) + (Y - 1) + 1 + (Z - 1) * Y + Z * (Y - 1)
    sems = {
        "w_s": (8,),
        "seg_s": (2,),
        "t_s": (6,),
        "xr_s": (2, n - 1),
        "xr_r": (2, n - 1),
        "xd_s": (3, n - 1),
        "xd_r": (3, n - 1),
        "sw_s": (10, GN - 1),
        "sw_r": (10, GN - 1),
        "kv_s": (n_sends,),
        "kv_r": (S,),
        "q_s": (n_sends,),
        "q_r": (S,),
        "da_s": (n_sends,),
        "da_r": (S,),
        "st_s": (n_sends,),
        "st_r": (S,),
        "sm_s": (2,),
        "gs_s": (4,),
        "gs_r": (4,),
        "gy_s": (4, Y - 1),
        "gy_r": (4, Y - 1),
        "gz_s": (4, Z - 1),
        "gz_r": (4, Z - 1),
    }
    names = ins + list(outs) + list(vm) + list(sems)

    def kernel(*refs):
        r = SimpleNamespace(**dict(zip(names, refs, strict=True)))
        g = r.__dict__
        s = lax.axis_index("seq")
        m = lax.axis_index("mlp")
        c = lax.rem(s, 2)
        chip = s // 2
        y = lax.rem(chip, Y)
        z = chip // Y
        sib = s + 1 - 2 * c
        gi = lax.rem(s, GN)

        def rank(zz, yy, cc):
            return (zz * Y + yy) * 2 + cc

        def remote(src, dst, send, recv, seq, mlp):
            return pltpu.make_async_remote_copy(
                src_ref=src, dst_ref=dst, send_sem=send, recv_sem=recv, device_id=(seq, mlp), device_id_type=MESH
            )

        bar = pltpu.get_barrier_semaphore()

        def greet(i, carry):
            pl.semaphore_signal(bar, inc=1, device_id=(lax.rem(s + i, S), m), device_id_type=MESH)
            return carry

        lax.fori_loop(1, S, greet, 0)
        for j in range(1, n):

            def greet_other(i, carry, j=j):
                pl.semaphore_signal(bar, inc=1, device_id=(i * 2 + c, lax.rem(m + j, n)), device_id_type=MESH)
                return carry

            lax.fori_loop(0, ZY, greet_other, 0)
        loads = [
            pltpu.make_async_copy(src.at[b], dst.at[b], r.w_s.at[4 * b + i])
            for b in range(2)
            for i, (src, dst) in enumerate(
                ((r.qkv_h, r.wq), (r.proj_h, r.wp), (r.up_h, r.wu), (r.down_h, r.wd))
            )
        ]
        for load in loads:
            load.start()

        prow = jnp.concatenate([r.picks[i : i + 1, :] + G * i for i in range(groups)], axis=1)
        here = s * T + lax.broadcasted_iota(jnp.int32, (T, R), 0)
        hot = jnp.where(prow == here, 1.0, 0.0)
        r.oht[...] = hot.astype(BF)
        r.oh[...] = jnp.transpose(hot).astype(BF)
        prow_f = prow.astype(F32)
        for i in range(GN):
            r.posr[i] = jnp.broadcast_to(prow_f[:, i * RH : (i + 1) * RH], (8, RH))
        r.posc[...] = column(r.posr[gi][0:1])
        r.sega[s] = jnp.broadcast_to(r.segr[...], (8, T))
        r.segc[...] = column(r.segr[...])

        def my_columns(x):
            got = x[:, 0:DM]
            for j in range(1, n):
                got = jnp.where(m == j, x[:, j * DM : (j + 1) * DM], got)
            return got

        def scatter_rows(x):
            r.part[...] = nn(r.oh[...], my_columns(x)).astype(BF).reshape(S, RB, DM)

        scatter_rows(r.inp[...])
        pl.semaphore_wait(bar, S - 1 + (n - 1) * ZY)

        def send_segments(i, carry):
            remote(r.sega.at[s], r.sega.at[s], r.seg_s.at[0], r.seg_s.at[1], lax.rem(s + i, S), m).start()
            return carry

        lax.fori_loop(1, S, send_segments, 0)

        def spread_rows():
            sem = [r.t_s.at[j] for j in range(6)]

            def first(k, carry):
                p = lax.rem(s + k, S)
                remote(r.part.at[p], r.r1.at[s], sem[0], sem[1], p, m).start()
                return carry

            lax.fori_loop(1, S, first, 0)
            r.r1[s] = r.part[s]
            some = pl.ds(0, S - 1)
            remote(r.part.at[some], r.r1.at[some], sem[0], sem[1], s, m).wait()
            me = m * ZY + chip
            r.full[c, me] = jnp.sum(r.r1[...].astype(F32), axis=0).astype(BF)

            def second(k, carry):
                p = lax.rem(me + k, n * ZY)
                block = r.full.at[c, me]
                remote(block, block, sem[2], sem[3], lax.rem(p, ZY) * 2 + c, p // ZY).start()
                return carry

            lax.fori_loop(1, n * ZY, second, 0)
            some = r.full.at[c, pl.ds(0, n * ZY - 1)]
            remote(some, some, sem[2], sem[3], s, m).wait()
            swap = remote(r.full.at[c], r.full.at[c], sem[4], sem[5], sib, m)
            swap.start()
            swap.wait()

            def place(k, carry):
                for cc in range(2):
                    rows = pl.ds(pl.multiple_of((k * 2 + cc) * RB, RB), RB)
                    for mm in range(n):
                        r.rows[rows, mm * DM : (mm + 1) * DM] = r.full[cc, mm * ZY + k]
                return carry

            lax.fori_loop(0, ZY, place, 0)

        def mlp_copies(buf, send, recv, i):
            i = i % buf.shape[0]
            return [
                remote(buf.at[i, m], buf.at[i, m], send.at[i, j - 1], recv.at[i, j - 1], s, lax.rem(m + j, n))
                for j in range(1, n)
            ]

        def mlp_start(which, i, value):
            buf = g["x" + which]
            buf[i % buf.shape[0], m] = value.astype(BF)
            for copy in mlp_copies(buf, g["x" + which + "_s"], g["x" + which + "_r"], i):
                copy.start()

        def mlp_total(which, i):
            buf = g["x" + which]
            for copy in mlp_copies(buf, g["x" + which + "_s"], g["x" + which + "_r"], i):
                copy.wait()
            i = i % buf.shape[0]
            total = buf[i, 0].astype(F32)
            for j in range(1, n):
                total = total + buf[i, j].astype(F32)
            return total

        def friend(j):
            return s - gi + lax.rem(gi + j, GN)

        def share(i, *refs):
            return [
                remote(ref.at[gi], ref.at[gi], r.sw_s.at[i + k, j - 1], r.sw_r.at[i + k, j - 1], friend(j), m)
                for k, ref in enumerate(refs)
                for j in range(1, GN)
            ]

        def attend(count, pick, query, key, value, mask, top, total, acc):
            top[...] = jnp.full(top.shape, NEG, F32)
            total[...] = jnp.zeros(total.shape, F32)
            acc[...] = jnp.zeros(acc.shape, F32)

            def step(i, carry):
                ci = pick(i)
                kept = mask(ci)
                for h in range(H):
                    scores = jnp.where(kept, nt(query(h), key(ci, h)) * SCALE, NEG)
                    old = top[h]
                    new = jnp.maximum(old, jnp.max(scores, axis=-1, keepdims=True))
                    shrink = jnp.exp(old - new)
                    weights = jnp.exp(scores - new)
                    total[h] = total[h] * shrink + jnp.sum(weights, axis=-1, keepdims=True)
                    acc[h] = acc[h] * shrink + nn(weights.astype(BF), value(ci, h))
                    top[h] = new
                return carry

            lax.fori_loop(0, count, step, 0)

        def finish(top, total, acc, mixed):
            for h in range(H):
                out = acc[h] / total[h]
                acc[h] = out
                mixed[:, h * HD : (h + 1) * HD] = out.astype(BF)
                top[h] = top[h] + jnp.log(total[h])

        def row_stats(grad, top, total, acc):
            lane = lax.broadcasted_iota(jnp.int32, (acc.shape[1], 128), 1)
            stats = jnp.zeros((acc.shape[1], 128), F32)
            for h in range(H):
                delta = jnp.sum(grad(h).astype(F32) * acc[h], axis=-1, keepdims=True)
                total[h] = delta
                stats = jnp.where(lane == h, top[h], jnp.where(lane == 8 + h, delta, stats))
            return jnp.transpose(stats)[0:16]

        def back_query(count, pick, query, grad, key, value, mask, log_total, delta, out):
            out[...] = jnp.zeros(out.shape, F32)

            def step(i, carry):
                ci = pick(i)
                kept = mask(ci)
                for h in range(H):
                    scores = nt(query(h), key(ci, h)) * SCALE
                    probs = jnp.where(kept, jnp.exp(scores - log_total[h]), 0.0)
                    grad_probs = nt(grad(h), value(ci, h))
                    grad_scores = (probs * (grad_probs - delta[h])).astype(BF)
                    out[h] = out[h] + nn(grad_scores, key(ci, h))
                return carry

            lax.fori_loop(0, count, step, 0)

        def back_keys(count, pick, key, value, query, grad, mask, stat, out_key, out_value):
            out_key[...] = jnp.zeros(out_key.shape, F32)
            out_value[...] = jnp.zeros(out_value.shape, F32)

            def step(i, carry):
                ci = pick(i)
                kept = mask(ci)
                for h in range(H):
                    scores = nt(key(h), query(ci, h)) * SCALE
                    probs = jnp.where(kept, jnp.exp(scores - stat(ci, h)), 0.0)
                    out_value[h] = out_value[h] + nn(probs.astype(BF), grad(ci, h))
                    grad_probs = nt(value(h), grad(ci, h))
                    grad_scores = (probs * (grad_probs - stat(ci, 8 + h))).astype(BF)
                    out_key[h] = out_key[h] + nn(grad_scores, query(ci, h))
                return carry

            lax.fori_loop(0, count, step, 0)

        dq_d, dk_d, dv_d = (ref.at[:, 0:T] for ref in (r.dq, r.dk, r.dv))
        dq_r, dk_r, dv_r = (ref.at[:, 0:RH] for ref in (r.dq, r.dk, r.dv))

        def pack_grads(dq, dk, dv, out):
            for h in range(H):
                out[:, h * HD : (h + 1) * HD] = (dq[h] * SCALE).astype(BF)
                out[:, W + h * HD : W + (h + 1) * HD] = (dk[h] * SCALE).astype(BF)
                out[:, 2 * W + h * HD : 2 * W + (h + 1) * HD] = dv[h].astype(BF)

        def front_back(grads, b):
            return (
                nt(grads[:, 0:W], r.wq[b, 0])
                + nt(grads[:, W : 2 * W], r.wq[b, 1])
                + nt(grads[:, 2 * W : 3 * W], r.wq[b, 2])
            )

        def gather(items):
            sent = []
            at = [0]

            def send(cond, slot, dst, which):
                k = at[0]
                for buf, ss, rs, up in [items[w] for w in which]:

                    def copy(buf=buf, ss=ss, rs=rs):
                        return remote(buf.at[slot], buf.at[slot], ss.at[k], rs.at[slot], dst, m)

                    if cond is None:
                        copy().start()
                    else:
                        pl.when(cond)(lambda copy=copy: copy().start())
                    sent.append((cond, copy))
                at[0] += 1

            def recv(slot, which):
                for buf, ss, rs, up in [items[w] for w in which]:
                    remote(buf.at[slot], buf.at[slot], ss.at[0], rs.at[slot], s, m).wait_recv()

            every = list(range(len(items)))
            ups = [w for w in every if items[w][3]]
            downs = [w for w in every if not items[w][3]]

            def start():
                for dz in range(1, Z):
                    k = at[0]
                    if ups:
                        send(z + dz < Z, s, rank(z + dz, y, c), ups)
                    if downs:
                        at[0] = k
                        send(z - dz >= 0, s, rank(z - dz, y, c), downs)
                    at[0] = k + 1
                for dy in range(1, Y):
                    send(None, s, rank(z, lax.rem(y + dy, Y), c), every)
                send(None, s, sib, every)

            def level():
                for dy in range(1, Y):
                    slot = rank(z, lax.rem(y + dy, Y), c)
                    recv(slot, every)
                    send(None, slot, sib, every)

            def relay(cond, slot, which, wide):
                pl.when(cond)(lambda: recv(slot, which))
                if wide:
                    for dy in range(1, Y):
                        send(cond, slot, rank(z, lax.rem(y + dy, Y), c), which)
                send(cond, slot, sib, which)

            def both(dz, body):
                k = at[0]
                end = k
                for sign, which in ((-1, ups), (1, downs)):
                    if which:
                        at[0] = k
                        zz = z + sign * dz
                        body((zz >= 0) & (zz < Z), zz, which)
                        end = at[0]
                at[0] = end

            def rest():
                for dz in range(1, Z):
                    both(dz, lambda cond, zz, which: relay(cond, rank(zz, y, c), which, True))
                for dz in range(1, Z):
                    for dy in range(1, Y):
                        yy = lax.rem(y + dy, Y)
                        both(dz, lambda cond, zz, which: relay(cond, rank(zz, yy, c), which, False))
                for dy in range(Y):
                    recv(rank(z, lax.rem(y + dy, Y), 1 - c), every)
                for dz in range(1, Z):
                    for dy in range(Y):
                        yy = lax.rem(y + dy, Y)

                        def last(cond, zz, which):
                            pl.when(cond)(lambda: recv(rank(zz, yy, 1 - c), which))

                        both(dz, last)

            def end():
                for cond, copy in sent:
                    if cond is None:
                        copy().wait_send()
                    else:
                        pl.when(cond)(lambda copy=copy: copy().wait_send())

            return SimpleNamespace(start=start, level=level, rest=rest, end=end)

        for par in range(2):
            ids = lax.broadcasted_iota(jnp.int32, (D, Q), 0)
            r.sele[par] = jnp.where(ids == r.target[par], 1.0, 0.0).astype(BF)

        def sum_start(k, lhs, rhs):
            i = KINDS.index(k)
            out = nn(lhs[...], r.sele[1 - c]).astype(BF)
            stay = nn(lhs[...], r.sele[c]).astype(BF)
            for x, w in chunks(XW[k]):
                g["send_" + k][:, :, :, x : x + w] = tn(out, rhs[:, x : x + w]).astype(BF).reshape(Y, Z, DRP, w)
            remote(g["send_" + k], g["sibr_" + k], r.gs_s.at[i], r.gs_r.at[i], sib, m).start()
            for x, w in chunks(XW[k]):
                g["keep_" + k][:, :, :, x : x + w] = tn(stay, rhs[:, x : x + w]).reshape(Y, Z, DRP, w)

        def y_copy(k, i, dy):
            return remote(
                g["sibr_" + k].at[lax.rem(y + dy, Y)],
                g["yrec_" + k].at[dy - 1],
                r.gy_s.at[i, dy - 1],
                r.gy_r.at[i, dy - 1],
                rank(z, lax.rem(y + dy, Y), c),
                m,
            )

        def z_copy(k, i, dz):
            return remote(
                g["yrec_" + k].at[0, lax.rem(z + dz, Z)],
                g["zrec_" + k].at[dz - 1],
                r.gz_s.at[i, dz - 1],
                r.gz_r.at[i, dz - 1],
                rank(lax.rem(z + dz, Z), y, c),
                m,
            )

        def sum_y(k):
            i = KINDS.index(k)
            remote(g["send_" + k], g["sibr_" + k], r.gs_s.at[i], r.gs_r.at[i], sib, m).wait()
            for dy in range(1, Y):
                yy = lax.rem(y + dy, Y)
                g["sibr_" + k][yy] = (g["keep_" + k][yy] + g["sibr_" + k][yy].astype(F32)).astype(BF)
                y_copy(k, i, dy).start()

        def sum_z(k):
            i = KINDS.index(k)
            for dy in range(1, Y):
                y_copy(k, i, dy).wait()

            def total(zz):
                t = g["keep_" + k][y, zz] + g["sibr_" + k][y, zz].astype(F32)
                for dy in range(1, Y):
                    t = t + g["yrec_" + k][dy - 1, zz].astype(F32)
                return t

            for dz in range(1, Z):
                zz = lax.rem(z + dz, Z)
                g["yrec_" + k][0, zz] = total(zz).astype(BF)
                z_copy(k, i, dz).start()
            g["keep_" + k][y, z] = total(z)

        def put(b, k, value):
            if k == "qkv":
                for j in range(3):
                    r.qkv_o[b, j] = value[0:DR, j * W : (j + 1) * W]
            elif k == "up":
                r.up_o[b] = value[0:DR]
            else:
                g[k + "_o"][b] = jnp.transpose(value)[:, 0:DR]

        def sum_end(k):
            i = KINDS.index(k)
            t = g["keep_" + k][y, z]
            for dz in range(1, Z):
                z_copy(k, i, dz).wait()
                t = t + g["zrec_" + k][dz - 1].astype(F32)
            put(1, k, t)

        def routed_copy(k, j):
            i = 6 + KINDS.index(k)
            send, recv = r.sw_s.at[i, j - 1], r.sw_r.at[i, j - 1]
            return remote(g["rsend_" + k].at[j - 1], g["rrec_" + k].at[j - 1], send, recv, friend(j), m)

        def routed_start(k, lhs, rhs):
            col = lax.broadcasted_iota(jnp.int32, (D, DRP), 1)
            row = lax.broadcasted_iota(jnp.int32, (D, DRP), 0)

            def block(who):
                hit = (row - who * DR == col) & (col < DR)
                return nn(lhs, jnp.where(hit, 1.0, 0.0).astype(BF)).astype(BF)

            for j in range(1, GN):
                g["rsend_" + k][j - 1] = tn(block(friend(j)), rhs).astype(BF)
                routed_copy(k, j).start()
            g["rkeep_" + k][...] = tn(block(s), rhs)

        def routed_end(k):
            t = g["rkeep_" + k][...]
            for j in range(1, GN):
                routed_copy(k, j).wait()
                t = t + g["rrec_" + k][j - 1].astype(F32)
            put(0, k, t)

        def head(h):
            return slice(h * HD, (h + 1) * HD)

        spread_rows()
        some = pl.ds(0, S - 1)
        remote(r.sega.at[some], r.sega.at[some], r.seg_s.at[0], r.seg_s.at[1], s, m).wait()
        starts = [
            jnp.sum(
                jnp.sum(jnp.where(r.sega[...] < k, 0.125, 0.0), axis=0), axis=(0, 1), keepdims=True
            )
            for k in range(1, 5)
        ]
        for i in range(GN):
            r.sgr[i] = sum(jnp.where(r.posr[i] >= at, 1.0, 0.0) for at in starts)
        r.sgc[...] = sum(jnp.where(r.posc[...] >= at, 1.0, 0.0) for at in starts)
        half = pl.ds(pl.multiple_of(gi * RH, RH), RH)

        loads[0].wait()
        r.chh[...] = r.rows[half, :]
        r.nr[...] = rms(r.chh[...].astype(F32), r.gains[0, 0:1]).astype(BF)
        for at in range(0, R, 256):
            part = slice(at, at + 256)
            normed = rms(r.rows[part].astype(F32), r.gains[0, 0:1]).astype(BF)
            r.qr[part] = nn(normed, r.wq[0, 0]).astype(BF)
            r.kr[part] = nn(normed, r.wq[0, 1]).astype(BF)
            r.vr[part] = nn(normed, r.wq[0, 2]).astype(BF)

        def part_rows(ref):
            return lambda ci, h: ref[pl.ds(pl.multiple_of(ci * RH, RH), RH), head(h)]

        def half_rows(ref):
            return lambda h: ref[half, head(h)]

        def routed_mask(ci):
            return (r.sgr[ci][0:1] == r.sgc[...]) & (r.posr[ci][0:1] <= r.posc[...])

        def routed_mask_back(ci):
            return (r.sgr[ci][0:1] == r.sgc[...]) & (r.posc[...] <= r.posr[ci][0:1])

        def routed_pick(i):
            return lax.rem(gi + i, GN)

        attend(GN, routed_pick, half_rows(r.qr), part_rows(r.kr), part_rows(r.vr), routed_mask, r.mr, r.lr, r.ar)
        finish(r.mr, r.lr, r.ar, r.mixr)
        loads[1].wait()
        mlp_start("r", 0, nn(r.mixr[...], r.wp[0]))
        loads[2].wait()
        loads[3].wait()
        attn = mlp_total("r", 0)
        r.attr[...] = attn
        normed = rms(r.chh[...].astype(F32) + attn, r.gains[0, 1:2]).astype(BF)
        r.n2r[...] = normed
        for x, w in chunks(F):
            pre = nn(normed, r.wu[0, :, x : x + w])
            r.prer[:, x : x + w] = pre
            r.actr[:, x : x + w] = gelu_pair(pre)[0].astype(BF)
        mlp_start("r", 1, nn(r.actr[...], r.wd[0]))
        mlp = mlp_total("r", 1)
        r.chg[gi] = (r.attr[...] + mlp).astype(BF)
        swaps = share(0, r.chg)
        for copy in swaps:
            copy.start()
        inp = r.inp[...].astype(F32)
        gate = jax.nn.sigmoid(jnp.sum(inp * r.router[...], axis=-1, keepdims=True))
        for load in loads[4:]:
            load.wait()
        for copy in swaps:
            copy.wait()

        sel = nn(r.oht[...], r.chg[...].reshape(R, D))
        r.sel[...] = sel.astype(BF)
        ro = inp + gate * sel
        r.ro[...] = ro
        r.ro_o[...] = ro.astype(BF)
        normed = rms(ro, r.gains[1, 0:1]).astype(BF)
        r.nd[...] = normed
        r.kva[s, :, 0:W] = nn(normed, r.wq[1, 1]).astype(BF)
        r.kva[s, :, W : 2 * W] = nn(normed, r.wq[1, 2]).astype(BF)
        r.qa[s] = nn(normed, r.wq[1, 0]).astype(BF)
        spread = gather([(r.kva, r.kv_s, r.kv_r, True), (r.qa, r.q_s, r.q_r, False)])
        spread.start()
        spread.level()
        spread.rest()

        def level_rows(ref, first=0):
            def get(ci, h):
                return ref[pl.ds(ci * LEVEL, LEVEL), :, head(first + h)].reshape(CH, HD)

            return get

        def level_line(ref, line):
            return lambda ci: jnp.concatenate([ref[ci * LEVEL + j][line : line + 1] for j in range(LEVEL)], axis=1)

        own_pos = lax.broadcasted_iota(jnp.int32, (T, CH), 0) + s * T
        far_pos = lax.broadcasted_iota(jnp.int32, (T, CH), 1)
        seg_line = level_line(r.sega, 0)

        def dense_mask(ci):
            return (seg_line(ci).astype(F32) == r.segc[...]) & (far_pos + ci * CH <= own_pos)

        def dense_mask_back(ci):
            return (seg_line(ci).astype(F32) == r.segc[...]) & (own_pos <= far_pos + ci * CH)

        attend(
            z + 1,
            lambda i: z - i,
            lambda h: r.qa[s, :, head(h)],
            level_rows(r.kva, 0),
            level_rows(r.kva, H),
            dense_mask,
            r.md,
            r.ld,
            r.ad,
        )
        finish(r.md, r.ld, r.ad, r.mixd)
        mlp_start("d", 0, nn(r.mixd[...], r.wp[1]))
        for x, w in chunks(F):
            r.dact[:, x : x + w] = nt(r.cot[...], r.wd[1, x : x + w, :])
        attn = mlp_total("d", 0)
        hid = r.ro[...] + attn
        r.hid[...] = hid
        normed = rms(hid, r.gains[1, 1:2]).astype(BF)
        r.n2d[...] = normed
        for x, w in chunks(F):
            active, slope = gelu_pair(nn(normed, r.wu[1, :, x : x + w]))
            r.actd[:, x : x + w] = active.astype(BF)
            r.dpre[:, x : x + w] = (r.dact[:, x : x + w] * slope).astype(BF)
        mlp_start("d", 1, nt(r.dpre[...], r.wu[1]))
        mlp_start("d", 2, nn(r.actd[...], r.wd[1]))

        sum_start("down", r.cot, r.actd)
        sum_start("up", r.n2d, r.dpre)
        dn, dg = rms_back(mlp_total("d", 1), r.hid[...], r.gains[1, 1:2])
        r.small[1:2] = dg
        dhid = r.cot[...].astype(F32) + dn
        r.dro[...] = dhid
        r.dattn[...] = dhid.astype(BF)
        r.da[s] = nt(r.dattn[...], r.wp[1]).astype(BF)
        r.sta[s] = row_stats(lambda h: r.da[s, :, head(h)], r.md, r.ld, r.ad)
        spread_back = gather([(r.da, r.da_s, r.da_r, False), (r.sta, r.st_s, r.st_r, False)])
        spread_back.start()
        spread_back.level()
        back_query(
            z + 1,
            lambda i: z - i,
            lambda h: r.qa[s, :, head(h)],
            lambda h: r.da[s, :, head(h)],
            level_rows(r.kva, 0),
            level_rows(r.kva, H),
            dense_mask,
            r.md,
            r.ld,
            dq_d,
        )
        spread_back.rest()
        back_keys(
            Z - z,
            lambda i: z + i,
            lambda h: r.kva[s, :, head(h)],
            lambda h: r.kva[s, :, head(H + h)],
            level_rows(r.qa),
            level_rows(r.da),
            dense_mask_back,
            lambda ci, line: level_line(r.sta, line)(ci),
            dk_d,
            dv_d,
        )
        pack_grads(dq_d, dk_d, dv_d, r.g3)
        mlp_start("d", 3, front_back(r.g3, 1))
        sum_start("proj", r.dattn, r.mixd)
        sum_start("qkv", r.nd, r.g3)
        sum_y("down")
        dn, dg = rms_back(mlp_total("d", 3), r.ro[...], r.gains[1, 0:1])
        r.small[0:1] = dg
        dro = r.dro[...] + dn
        r.dro[...] = dro

        sel = r.sel[...].astype(F32)
        inp = r.inp[...].astype(F32)
        gate = jax.nn.sigmoid(jnp.sum(inp * r.router[...], axis=-1, keepdims=True))
        dlogit = jnp.sum(dro * sel, axis=-1, keepdims=True) * gate * (1.0 - gate)
        scatter_rows((gate * dro).astype(BF))
        spread_rows()
        r.small[2:3] = jnp.sum(inp * dlogit, axis=0, keepdims=True)
        r.small[3:8] = jnp.zeros((5, D), F32)
        r.sblk[...] = jnp.zeros((S, 8, 128), F32)
        for p in range(S):
            r.sblk[p, :, 0:DR] = r.small[:, p * DR : (p + 1) * DR]

        def send_small(i, carry):
            p = lax.rem(s + i, S)
            remote(r.sblk.at[p], r.srec.at[s], r.sm_s.at[0], r.sm_s.at[1], p, m).start()
            return carry

        lax.fori_loop(1, S, send_small, 0)
        r.srec[s] = r.sblk[s]

        dmlp = r.rows[half, :]
        r.attr[...] = r.attr[...] + r.chh[...].astype(F32)
        for x, w in chunks(F):
            grad_active = nt(dmlp, r.wd[0, x : x + w, :])
            r.dprer[:, x : x + w] = (grad_active * gelu_pair(r.prer[:, x : x + w])[1]).astype(BF)
        mlp_start("r", 2, nt(r.dprer[...], r.wu[0]))
        routed_start("down", dmlp, r.actr[...])
        routed_start("up", r.n2r[...], r.dprer[...])
        dn, dg2 = rms_back(mlp_total("r", 2), r.attr[...], r.gains[0, 1:2])
        r.attr[...] = dn
        r.dattr[...] = (dmlp.astype(F32) + dn).astype(BF)
        r.dor[gi] = nt(r.dattr[...], r.wp[0]).astype(BF)
        r.str[gi] = row_stats(lambda h: r.dor[gi, :, head(h)], r.mr, r.lr, r.ar)
        swaps = share(1, r.dor, r.str)
        for copy in swaps:
            copy.start()
        routed_start("proj", r.dattr[...], r.mixr[...])
        back_query(
            GN,
            routed_pick,
            half_rows(r.qr),
            lambda h: r.dor[gi, :, head(h)],
            part_rows(r.kr),
            part_rows(r.vr),
            routed_mask,
            r.mr,
            r.lr,
            dq_r,
        )
        for copy in swaps:
            copy.wait()
        back_keys(
            GN,
            routed_pick,
            half_rows(r.kr),
            half_rows(r.vr),
            part_rows(r.qr),
            lambda ci, h: r.dor[ci, :, head(h)],
            routed_mask_back,
            lambda ci, line: r.str[ci][line : line + 1],
            dk_r,
            dv_r,
        )
        pack_grads(dq_r, dk_r, dv_r, r.g3r)
        mlp_start("r", 3, front_back(r.g3r, 0))
        routed_start("qkv", r.nr[...], r.g3r[...])
        sum_y("up")
        sum_y("proj")
        sum_y("qkv")
        sum_z("down")
        dn, dg1 = rms_back(mlp_total("r", 3), r.chh[...].astype(F32), r.gains[0, 0:1])
        r.chg[gi] = (r.attr[...] + dn).astype(BF)
        r.gr[gi] = jnp.concatenate([dg1, dg2, jnp.zeros((6, D), F32)], axis=0)
        swaps = share(3, r.chg, r.gr)
        for copy in swaps:
            copy.start()
        for copy in swaps:
            copy.wait()
        r.rg_o[...] = jnp.sum(r.gr[...], axis=0)[0:2]
        back = nn(r.oht[...], r.chg[...].reshape(R, D))
        inp = r.inp[...].astype(F32)
        gate = jax.nn.sigmoid(jnp.sum(inp * r.router[...], axis=-1, keepdims=True))
        dlogit = jnp.sum(r.dro[...] * r.sel[...].astype(F32), axis=-1, keepdims=True) * gate * (1.0 - gate)
        r.gi_o[...] = r.dro[...] + back + dlogit * r.router[...]

        r.do_o[...] = (r.hid[...] + mlp_total("d", 2)).astype(BF)
        some = pl.ds(0, S - 1)
        remote(r.sblk.at[some], r.srec.at[some], r.sm_s.at[0], r.sm_s.at[1], s, m).wait()
        r.sm_o[...] = jnp.sum(r.srec[...], axis=0)
        for k in ("up", "proj", "qkv"):
            sum_z(k)
        for k in KINDS:
            routed_end(k)
        for k in KINDS:
            sum_end(k)
        spread.end()
        spread_back.end()

    def run(inp, segments, picks, gains, router, qkv, proj, up, down, cot):
        args = (
            inp,
            segments.reshape(1, T),
            picks,
            gains,
            router.reshape(1, D),
            cot,
            jnp.asarray(target),
            qkv,
            proj,
            up,
            down,
        )
        vmem = pl.BlockSpec(memory_space=pltpu.VMEM)
        hbm = pl.BlockSpec(memory_space=pl.ANY)
        res = pl.pallas_call(
            kernel,
            out_shape=[jax.ShapeDtypeStruct(sh, dt) for sh, dt in outs.values()],
            in_specs=[vmem] * 7 + [hbm] * 4,
            out_specs=[vmem] * len(outs),
            scratch_shapes=[pltpu.VMEM(sh, dt) for sh, dt in vm.values()] + [DMA(sh) for sh in sems.values()],
            compiler_params=pltpu.CompilerParams(
                collective_id=0, has_side_effects=True, vmem_limit_bytes=62 * 1024 * 1024
            ),
            name="train_step",
        )(*args)
        ro, do, gi, sm, rg, gq, gp, gu, gd = res
        at = lax.axis_index("seq") * DR
        routed_gains = lax.dynamic_slice_in_dim(rg, at, DR, 1)
        gains_grad = jnp.stack([routed_gains, sm[0:2, 0:DR]])
        return (ro, do, gi, gains_grad, sm[2, 0:DR], gq, gp, gu, gd)

    return run


def solution(mesh):
    S, n = mesh.shape["seq"], mesh.shape["mlp"]

    def body(inp, segments, picks, gains, router, qkv, proj, up, down, cot):
        run = build(
            S, n, inp.shape[0], inp.shape[1], qkv.shape[-1], up.shape[-1], picks.size, picks.shape[0]
        )
        return run(inp, segments, picks, gains, router, qkv, proj, up, down, cot)

    return jax.shard_map(
        body,
        mesh=mesh,
        in_specs=(
            P("seq", None),
            P("seq"),
            P(),
            P(),
            P(),
            P(None, None, None, "mlp"),
            P(None, "mlp", None),
            P(None, None, "mlp"),
            P(None, "mlp", None),
            P("seq", None),
        ),
        out_specs=(
            P("seq", None),
            P("seq", None),
            P("seq", None),
            P(None, None, "seq"),
            P("seq"),
            P(None, None, "seq", "mlp"),
            P(None, "mlp", "seq"),
            P(None, "seq", "mlp"),
            P(None, "mlp", "seq"),
        ),
        check_vma=False,
    )
```

time: 1080 us -> 226 us (0.21); the launches traced: 1070 us -> 226 us
  waiting for transfers between devices: 643 us -> 0 us
  Pallas kernels: 0 us -> 212 us
  blocking collectives: 168 us -> 0 us
  matrix products: 103 us -> 0 us
  local copies, waits for them, and re-layouts: 64.5 us -> 13.3 us
  other arithmetic: 47 us -> 0.58 us
  starting transfers between devices: 24.2 us -> 0 us
  between operations: 18.7 us -> 0.69 us
    reduce_scatter x3 -> x0, waiting for transfers between devices: 268 us -> none  [the longest x1 115 us: body(): lax.psum_scatter(jnp.stack([grad_up_r, grad_up_d]), 'seq', scatter_dimens...]
    unnamed x12 -> x0, waiting for transfers between devices: 219 us -> none
    pallas_call x0 -> x1, Pallas kernels: none -> 212 us  [run(): pl.pallas_call(kernel, out_shape=[jax.ShapeDtypeStruct(sh, dt) for sh, dt...]
    dot_general x55 -> x0, matrix products: 103 us -> none  [the longest x12 22.8 us: contract_cols(): lax.dot_general(left, right, (((1,), (1,)), ((), ())), preferred_element_...]
    psum x3 -> x0, waiting for transfers between devices: 80.4 us -> none  [unit_total(): return lax.psum(term, 'mlp')]
    unnamed x2 -> x0, blocking collectives: 79.4 us -> none
    all_gather x3 -> x0, blocking collectives: 55.5 us -> none  [the longest x1 18.8 us: body(): lax.all_gather(values_one, 'seq', axis=0, tiled=True)]
    all_gather x2 -> x0, waiting for transfers between devices: 53.7 us -> none  [the longest x1 41.4 us: body(): lax.all_gather(values_dense, 'seq', axis=0, tiled=True)]
  transfers between devices with their start and end apart: 15 -> 0, of which waited for: 14 -> 0; matrix products, arithmetic and copies ran while one was open for 9% -> 0% of each run, Pallas kernels for 0% -> 0%
where the time goes in v1:
time: 226 us
  Pallas kernels  212 us (94%)
  local copies, waits for them, and re-layouts  13.3 us (6%)
    pallas_call x1, Pallas kernels, run(): pl.pallas_call(kernel, out_shape=[jax.ShapeDtypeStruct(sh, dt) for sh, dt...  212 us
    unnamed x13, local copies, waits for them, and re-layouts  10 us

profile of v1, /device:TPU:0, one launch (start us, length us, event | category | flops | bytes accessed | tf_op | source)
XLA Modules:
  0.0 226.1 jit_solution(14183819169136505079)
XLA Ops:
  0.6 1.3 reshape.25.refs_4_
  1.9 211.5 %train_step.1 = (bf16[128,768]{1,0:T(8,128)(2,1)}, bf16[128,768]{1,0:T(8,128)(2,1)}, f32[128,768]{1,0:T(8,128)}, f32[8,128]{1,0:T(8,128)}, f32[2,768]{1,0:T(2,12...) custom-call(bf16[128,768]{1,0:T(8,128)(2,1)} %refs_0_.1, ...), custom_call_target="tpu_custom_call" | custom-call | tf_op jit(solution)/shard_map/train_step/pallas_call | solution.py:927
  213.5 0.0 copy-start.2
  213.5 0.0 copy-start.1
  213.5 0.0 copy-start
  213.5 1.3 slice_bitcast_fusion.1
  214.8 0.7 slice_bitcast_fusion
  215.5 0.6 pad_maximum_fusion
  216.1 1.8 copy.20
  217.9 2.7 %copy.21 = f32[2,1536,48]{1,2,0:T(8,128)} copy(f32[2,1536,48]{2,1,0:T(8,128)} %get-tuple-element.35) | data formatting | bytes 1179648
  220.6 1.6 copy.27
  222.2 1.6 copy.28
  223.8 0.0 copy-done.2
  223.8 0.7 copy.29
  224.6 0.0 copy-done.1
  224.6 0.8 copy.30
  225.3 0.0 copy-done
  225.3 0.8 copy.31
Async XLA Ops:
  213.5 10.4 %copy-start.2 = (f32[128,768]{1,0:T(8,128)S(1)}, f32[128,768]{1,0:T(8,128)}, u32[]{:S(2)}) copy-start(f32[128,768]{1,0:T(8,128)} %get-tuple-element.49) | copy-start | bytes 1179652
  213.5 11.1 %copy-start.1 = (f32[2,3,48,384]{3,2,1,0:T(8,128)S(1)}, f32[2,3,48,384]{3,2,1,0:T(8,128)}, u32[]{:S(2)}) copy-start(f32[2,3,48,384]{3,2,1,0:T(8,128)} %get-tuple-element.52) | copy-start | bytes 1327108
  213.5 11.9 %copy-start = (f32[2,48,1536]{2,1,0:T(8,128)S(1)}, f32[2,48,1536]{2,1,0:T(8,128)}, u32[]{:S(2)}) copy-start(f32[2,48,1536]{2,1,0:T(8,128)} %get-tuple-element.54) | copy-start | bytes 1769476

commit v2 on v1

--- a/solution.py
+++ b/solution.py
@@ -19,6 +19,7 @@
 DMA = pltpu.SemaphoreType.DMA
 GELU_A = 0.044715
 GELU_B = float(np.sqrt(2.0 / np.pi))
+WIDE = 1536
 KINDS = ("down", "up", "proj", "qkv")
 
 
@@ -102,9 +103,9 @@
         "sm_o": ((8, 128), F32),
         "rg_o": ((2, D), F32),
         "qkv_o": ((2, 3, DR, W), F32),
-        "proj_o": ((2, W, DR), F32),
+        "proj_o": ((2, DR, W), F32),
         "up_o": ((2, DR, F), F32),
-        "down_o": ((2, F, DR), F32),
+        "down_o": ((2, DR, F), F32),
     }
     vm = {
         "wq": ((2, 3, D, W), BF),
@@ -115,9 +116,9 @@
         "segc": ((T, 1), F32),
         "oht": ((T, R), BF),
         "oh": ((R, T), BF),
-        "posr": ((GN, 8, RH), F32),
+        "posr": ((GN // 2, 8, 2 * RH), F32),
         "posc": ((RH, 1), F32),
-        "sgr": ((GN, 8, RH), F32),
+        "sgr": ((GN // 2, 8, 2 * RH), F32),
         "sgc": ((RH, 1), F32),
         "part": ((S, RB, DM), BF),
         "r1": ((S, RB, DM), BF),
@@ -252,20 +253,11 @@
                 ((r.qkv_h, r.wq), (r.proj_h, r.wp), (r.up_h, r.wu), (r.down_h, r.wd))
             )
         ]
-        for load in loads:
-            load.start()
-
         prow = jnp.concatenate([r.picks[i : i + 1, :] + G * i for i in range(groups)], axis=1)
         here = s * T + lax.broadcasted_iota(jnp.int32, (T, R), 0)
         hot = jnp.where(prow == here, 1.0, 0.0)
         r.oht[...] = hot.astype(BF)
         r.oh[...] = jnp.transpose(hot).astype(BF)
-        prow_f = prow.astype(F32)
-        for i in range(GN):
-            r.posr[i] = jnp.broadcast_to(prow_f[:, i * RH : (i + 1) * RH], (8, RH))
-        r.posc[...] = column(r.posr[gi][0:1])
-        r.sega[s] = jnp.broadcast_to(r.segr[...], (8, T))
-        r.segc[...] = column(r.segr[...])
 
         def my_columns(x):
             got = x[:, 0:DM]
@@ -277,17 +269,13 @@
             r.part[...] = nn(r.oh[...], my_columns(x)).astype(BF).reshape(S, RB, DM)
 
         scatter_rows(r.inp[...])
-        pl.semaphore_wait(bar, S - 1 + (n - 1) * ZY)
-
         def send_segments(i, carry):
             remote(r.sega.at[s], r.sega.at[s], r.seg_s.at[0], r.seg_s.at[1], lax.rem(s + i, S), m).start()
             return carry
 
-        lax.fori_loop(1, S, send_segments, 0)
-
-        def spread_rows():
-            sem = [r.t_s.at[j] for j in range(6)]
-
+        sem = [r.t_s.at[j] for j in range(6)]
+
+        def spread_start():
             def first(k, carry):
                 p = lax.rem(s + k, S)
                 remote(r.part.at[p], r.r1.at[s], sem[0], sem[1], p, m).start()
@@ -295,6 +283,8 @@
 
             lax.fori_loop(1, S, first, 0)
             r.r1[s] = r.part[s]
+
+        def spread_end(after):
             some = pl.ds(0, S - 1)
             remote(r.part.at[some], r.r1.at[some], sem[0], sem[1], s, m).wait()
             me = m * ZY + chip
@@ -307,6 +297,7 @@
                 return carry
 
             lax.fori_loop(1, n * ZY, second, 0)
+            after()
             some = r.full.at[c, pl.ds(0, n * ZY - 1)]
             remote(some, some, sem[2], sem[3], s, m).wait()
             swap = remote(r.full.at[c], r.full.at[c], sem[4], sem[5], sib, m)
@@ -355,26 +346,32 @@
                 for j in range(1, GN)
             ]
 
-        def attend(count, pick, query, key, value, mask, top, total, acc):
+        def attend_start(top, total, acc):
             top[...] = jnp.full(top.shape, NEG, F32)
             total[...] = jnp.zeros(total.shape, F32)
             acc[...] = jnp.zeros(acc.shape, F32)
 
-            def step(i, carry):
-                ci = pick(i)
-                kept = mask(ci)
-                for h in range(H):
-                    scores = jnp.where(kept, nt(query(h), key(ci, h)) * SCALE, NEG)
+        def head_groups(width):
+            step = min(H, max(1, WIDE // width))
+            return [range(at, min(at + step, H)) for at in range(0, H, step)]
+
+        def attend(ci, query, key, value, mask, top, total, acc):
+            kept = mask(ci)
+            for group in head_groups(kept.shape[1]):
+                scores = {h: nt(query(h), key(ci, h)) for h in group}
+                weights = {}
+                for h in group:
+                    score = jnp.where(kept, scores[h], NEG)
                     old = top[h]
-                    new = jnp.maximum(old, jnp.max(scores, axis=-1, keepdims=True))
+                    new = jnp.maximum(old, jnp.max(score, axis=-1, keepdims=True))
                     shrink = jnp.exp(old - new)
-                    weights = jnp.exp(scores - new)
-                    total[h] = total[h] * shrink + jnp.sum(weights, axis=-1, keepdims=True)
-                    acc[h] = acc[h] * shrink + nn(weights.astype(BF), value(ci, h))
+                    weight = jnp.exp(score - new)
+                    total[h] = total[h] * shrink + jnp.sum(weight, axis=-1, keepdims=True)
+                    acc[h] = acc[h] * shrink
                     top[h] = new
-                return carry
-
-            lax.fori_loop(0, count, step, 0)
+                    weights[h] = weight.astype(BF)
+                for h in group:
+                    acc[h] = acc[h] + nn(weights[h], value(ci, h))
 
         def finish(top, total, acc, mixed):
             for h in range(H):
@@ -392,39 +389,31 @@
                 stats = jnp.where(lane == h, top[h], jnp.where(lane == 8 + h, delta, stats))
             return jnp.transpose(stats)[0:16]
 
-        def back_query(count, pick, query, grad, key, value, mask, log_total, delta, out):
-            out[...] = jnp.zeros(out.shape, F32)
-
-            def step(i, carry):
-                ci = pick(i)
-                kept = mask(ci)
-                for h in range(H):
-                    scores = nt(query(h), key(ci, h)) * SCALE
-                    probs = jnp.where(kept, jnp.exp(scores - log_total[h]), 0.0)
-                    grad_probs = nt(grad(h), value(ci, h))
-                    grad_scores = (probs * (grad_probs - delta[h])).astype(BF)
-                    out[h] = out[h] + nn(grad_scores, key(ci, h))
-                return carry
-
-            lax.fori_loop(0, count, step, 0)
-
-        def back_keys(count, pick, key, value, query, grad, mask, stat, out_key, out_value):
-            out_key[...] = jnp.zeros(out_key.shape, F32)
-            out_value[...] = jnp.zeros(out_value.shape, F32)
-
-            def step(i, carry):
-                ci = pick(i)
-                kept = mask(ci)
-                for h in range(H):
-                    scores = nt(key(h), query(ci, h)) * SCALE
-                    probs = jnp.where(kept, jnp.exp(scores - stat(ci, h)), 0.0)
-                    out_value[h] = out_value[h] + nn(probs.astype(BF), grad(ci, h))
-                    grad_probs = nt(value(h), grad(ci, h))
-                    grad_scores = (probs * (grad_probs - stat(ci, 8 + h))).astype(BF)
-                    out_key[h] = out_key[h] + nn(grad_scores, query(ci, h))
-                return carry
-
-            lax.fori_loop(0, count, step, 0)
+        def back_query(ci, query, grad, key, value, mask, log_total, delta, out):
+            kept = mask(ci)
+            for group in head_groups(kept.shape[1]):
+                scores = {h: nt(query(h), key(ci, h)) for h in group}
+                grad_probs = {h: nt(grad(h), value(ci, h)) for h in group}
+                grad_scores = {}
+                for h in group:
+                    probs = jnp.where(kept, jnp.exp(scores[h] - log_total[h]), 0.0)
+                    grad_scores[h] = (probs * (grad_probs[h] - delta[h])).astype(BF)
+                for h in group:
+                    out[h] = out[h] + nn(grad_scores[h], key(ci, h))
+
+        def back_keys(ci, key, value, query, grad, mask, stat, out_key, out_value):
+            kept = mask(ci)
+            for group in head_groups(kept.shape[1]):
+                scores = {h: nt(key(h), query(ci, h)) for h in group}
+                grad_probs = {h: nt(value(h), grad(ci, h)) for h in group}
+                probs, grad_scores = {}, {}
+                for h in group:
+                    prob = jnp.where(kept, jnp.exp(scores[h] - stat(ci, h)), 0.0)
+                    grad_scores[h] = (prob * (grad_probs[h] - stat(ci, 8 + h))).astype(BF)
+                    probs[h] = prob.astype(BF)
+                for h in group:
+                    out_value[h] = out_value[h] + nn(probs[h], grad(ci, h))
+                    out_key[h] = out_key[h] + nn(grad_scores[h], query(ci, h))
 
         dq_d, dk_d, dv_d = (ref.at[:, 0:T] for ref in (r.dq, r.dk, r.dv))
         dq_r, dk_r, dv_r = (ref.at[:, 0:RH] for ref in (r.dq, r.dk, r.dv))
@@ -432,7 +421,7 @@
         def pack_grads(dq, dk, dv, out):
             for h in range(H):
                 out[:, h * HD : (h + 1) * HD] = (dq[h] * SCALE).astype(BF)
-                out[:, W + h * HD : W + (h + 1) * HD] = (dk[h] * SCALE).astype(BF)
+                out[:, W + h * HD : W + (h + 1) * HD] = dk[h].astype(BF)
                 out[:, 2 * W + h * HD : 2 * W + (h + 1) * HD] = dv[h].astype(BF)
 
         def front_back(grads, b):
@@ -442,99 +431,116 @@
                 + nt(grads[:, 2 * W : 3 * W], r.wq[b, 2])
             )
 
-        def gather(items):
-            sent = []
-            at = [0]
-
-            def send(cond, slot, dst, which):
-                k = at[0]
-                for buf, ss, rs, up in [items[w] for w in which]:
-
-                    def copy(buf=buf, ss=ss, rs=rs):
-                        return remote(buf.at[slot], buf.at[slot], ss.at[k], rs.at[slot], dst, m)
-
-                    if cond is None:
-                        copy().start()
-                    else:
-                        pl.when(cond)(lambda copy=copy: copy().start())
-                    sent.append((cond, copy))
-                at[0] += 1
-
-            def recv(slot, which):
-                for buf, ss, rs, up in [items[w] for w in which]:
-                    remote(buf.at[slot], buf.at[slot], ss.at[0], rs.at[slot], s, m).wait_recv()
-
-            every = list(range(len(items)))
-            ups = [w for w in every if items[w][3]]
-            downs = [w for w in every if not items[w][3]]
+        def loop(low, high, body):
+            def step(i, carry):
+                body(i)
+                return carry
+
+            lax.fori_loop(low, high, step, 0)
+
+        def gather(buf, ss, rs, up):
+            sign = -1 if up else 1
+            last = z if up else Z - 1 - z
+            ahead = Z - 1 - z if up else z
+            at_y, at_sib, at_level = Z - 1, Z + Y - 2, Z + Y - 1
+            at_z = at_level + Y - 1
+            at_far = at_z + (Z - 1) * Y
+
+            def copy(slot, dst, k):
+                return remote(buf.at[slot], buf.at[slot], ss.at[k], rs.at[slot], dst, m)
+
+            def recv(slot):
+                copy(slot, sib, 0).wait_recv()
+
+            def side(dy):
+                return lax.rem(y + dy, Y)
+
+            def copies(each):
+                loop(1, ahead + 1, lambda dz: each(copy(s, rank(z - sign * dz, y, c), dz - 1)))
+                for dy in range(1, Y):
+                    each(copy(s, rank(z, side(dy), c), at_y + dy - 1))
+                each(copy(s, sib, at_sib))
+
+            def level_copy(dy):
+                return copy(rank(z, side(dy), c), sib, at_level + dy - 1)
+
+            def z_copies(dz):
+                slot = rank(z + sign * dz, y, c)
+                k = at_z + (dz - 1) * Y
+                outs = [copy(slot, rank(z, side(dy), c), k + dy - 1) for dy in range(1, Y)]
+                return [*outs, copy(slot, sib, k + Y - 1)]
+
+            def far_copy(dz, dy):
+                return copy(rank(z + sign * dz, side(dy), c), sib, at_far + (dz - 1) * (Y - 1) + dy - 1)
 
             def start():
-                for dz in range(1, Z):
-                    k = at[0]
-                    if ups:
-                        send(z + dz < Z, s, rank(z + dz, y, c), ups)
-                    if downs:
-                        at[0] = k
-                        send(z - dz >= 0, s, rank(z - dz, y, c), downs)
-                    at[0] = k + 1
-                for dy in range(1, Y):
-                    send(None, s, rank(z, lax.rem(y + dy, Y), c), every)
-                send(None, s, sib, every)
+                copies(lambda one: one.start())
 
             def level():
                 for dy in range(1, Y):
-                    slot = rank(z, lax.rem(y + dy, Y), c)
-                    recv(slot, every)
-                    send(None, slot, sib, every)
-
-            def relay(cond, slot, which, wide):
-                pl.when(cond)(lambda: recv(slot, which))
-                if wide:
+                    recv(rank(z, side(dy), c))
+                    level_copy(dy).start()
+
+            def level_end():
+                for dy in range(Y):
+                    recv(rank(z, side(dy), 1 - c))
+
+            def z_step(dz):
+                recv(rank(z + sign * dz, y, c))
+                for one in z_copies(dz):
+                    one.start()
+
+            def y_step(dz):
+                for dy in range(1, Y):
+                    recv(rank(z + sign * dz, side(dy), c))
+                    far_copy(dz, dy).start()
+
+            def sib_step(dz):
+                for dy in range(Y):
+                    recv(rank(z + sign * dz, side(dy), 1 - c))
+
+            def end():
+                copies(lambda one: one.wait_send())
+                for dy in range(1, Y):
+                    level_copy(dy).wait_send()
+
+                def sent(dz):
+                    for one in z_copies(dz):
+                        one.wait_send()
                     for dy in range(1, Y):
-                        send(cond, slot, rank(z, lax.rem(y + dy, Y), c), which)
-                send(cond, slot, sib, which)
-
-            def both(dz, body):
-                k = at[0]
-                end = k
-                for sign, which in ((-1, ups), (1, downs)):
-                    if which:
-                        at[0] = k
-                        zz = z + sign * dz
-                        body((zz >= 0) & (zz < Z), zz, which)
-                        end = at[0]
-                at[0] = end
-
-            def rest():
-                for dz in range(1, Z):
-                    both(dz, lambda cond, zz, which: relay(cond, rank(zz, y, c), which, True))
-                for dz in range(1, Z):
-                    for dy in range(1, Y):
-                        yy = lax.rem(y + dy, Y)
-                        both(dz, lambda cond, zz, which: relay(cond, rank(zz, yy, c), which, False))
-                for dy in range(Y):
-                    recv(rank(z, lax.rem(y + dy, Y), 1 - c), every)
-                for dz in range(1, Z):
-                    for dy in range(Y):
-                        yy = lax.rem(y + dy, Y)
-
-                        def last(cond, zz, which):
-                            pl.when(cond)(lambda: recv(rank(zz, yy, 1 - c), which))
-
-                        both(dz, last)
-
-            def end():
-                for cond, copy in sent:
-                    if cond is None:
-                        copy().wait_send()
-                    else:
-                        pl.when(cond)(lambda copy=copy: copy().wait_send())
-
-            return SimpleNamespace(start=start, level=level, rest=rest, end=end)
-
-        for par in range(2):
-            ids = lax.broadcasted_iota(jnp.int32, (D, Q), 0)
-            r.sele[par] = jnp.where(ids == r.target[par], 1.0, 0.0).astype(BF)
+                        far_copy(dz, dy).wait_send()
+
+                loop(1, last + 1, sent)
+
+            return SimpleNamespace(
+                start=start,
+                level=level,
+                level_end=level_end,
+                z_step=z_step,
+                y_step=y_step,
+                sib_step=sib_step,
+                end=end,
+                last=last,
+            )
+
+        def walk(items, body):
+            last = items[0].last
+
+            def all_of(name, *args):
+                for item in items:
+                    getattr(item, name)(*args)
+
+            pl.when(last > 0)(lambda: all_of("z_step", 1))
+            all_of("level_end")
+            body(0)
+
+            def step(dz):
+                all_of("y_step", dz)
+                pl.when(dz < last)(lambda: all_of("z_step", dz + 1))
+                all_of("sib_step", dz)
+                body(dz)
+
+            loop(1, last + 1, step)
 
         def sum_start(k, lhs, rhs):
             i = KINDS.index(k)
@@ -595,10 +601,8 @@
             if k == "qkv":
                 for j in range(3):
                     r.qkv_o[b, j] = value[0:DR, j * W : (j + 1) * W]
-            elif k == "up":
-                r.up_o[b] = value[0:DR]
             else:
-                g[k + "_o"][b] = jnp.transpose(value)[:, 0:DR]
+                g[k + "_o"][b] = value[0:DR]
 
         def sum_end(k):
             i = KINDS.index(k)
@@ -636,7 +640,21 @@
         def head(h):
             return slice(h * HD, (h + 1) * HD)
 
-        spread_rows()
+        pl.semaphore_wait(bar, S - 1 + (n - 1) * ZY)
+        spread_start()
+        r.sega[s] = jnp.broadcast_to(r.segr[...], (8, T))
+        for load in loads:
+            load.start()
+        prow_f = prow.astype(F32)
+        for i in range(GN // 2):
+            r.posr[i] = jnp.broadcast_to(prow_f[:, i * 2 * RH : (i + 1) * 2 * RH], (8, 2 * RH))
+        mine = r.posr[gi // 2][0:1]
+        r.posc[...] = column(jnp.where(lax.rem(gi, 2) == 0, mine[:, 0:RH], mine[:, RH : 2 * RH]))
+        r.segc[...] = column(r.segr[...])
+        for par in range(2):
+            ids = lax.broadcasted_iota(jnp.int32, (D, Q), 0)
+            r.sele[par] = jnp.where(ids == r.target[par], 1.0, 0.0).astype(BF)
+        spread_end(lambda: lax.fori_loop(1, S, send_segments, 0))
         some = pl.ds(0, S - 1)
         remote(r.sega.at[some], r.sega.at[some], r.seg_s.at[0], r.seg_s.at[1], s, m).wait()
         starts = [
@@ -645,7 +663,7 @@
             )
             for k in range(1, 5)
         ]
-        for i in range(GN):
+        for i in range(GN // 2):
             r.sgr[i] = sum(jnp.where(r.posr[i] >= at, 1.0, 0.0) for at in starts)
         r.sgc[...] = sum(jnp.where(r.posc[...] >= at, 1.0, 0.0) for at in starts)
         half = pl.ds(pl.multiple_of(gi * RH, RH), RH)
@@ -656,12 +674,12 @@
         for at in range(0, R, 256):
             part = slice(at, at + 256)
             normed = rms(r.rows[part].astype(F32), r.gains[0, 0:1]).astype(BF)
-            r.qr[part] = nn(normed, r.wq[0, 0]).astype(BF)
+            r.qr[part] = (nn(normed, r.wq[0, 0]).astype(BF) * SCALE).astype(BF)
             r.kr[part] = nn(normed, r.wq[0, 1]).astype(BF)
             r.vr[part] = nn(normed, r.wq[0, 2]).astype(BF)
 
         def part_rows(ref):
-            return lambda ci, h: ref[pl.ds(pl.multiple_of(ci * RH, RH), RH), head(h)]
+            return lambda ci, h: ref[pl.ds(pl.multiple_of(ci * 2 * RH, RH), 2 * RH), head(h)]
 
         def half_rows(ref):
             return lambda h: ref[half, head(h)]
@@ -673,9 +691,20 @@
             return (r.sgr[ci][0:1] == r.sgc[...]) & (r.posc[...] <= r.posr[ci][0:1])
 
         def routed_pick(i):
-            return lax.rem(gi + i, GN)
-
-        attend(GN, routed_pick, half_rows(r.qr), part_rows(r.kr), part_rows(r.vr), routed_mask, r.mr, r.lr, r.ar)
+            return lax.rem(gi // 2 + i, GN // 2)
+
+        def routed_loop(body):
+            if GN == 2:
+                body(0)
+            else:
+                loop(0, GN // 2, lambda i: body(routed_pick(i)))
+
+        attend_start(r.mr, r.lr, r.ar)
+        routed_loop(
+            lambda ci: attend(
+                ci, half_rows(r.qr), part_rows(r.kr), part_rows(r.vr), routed_mask, r.mr, r.lr, r.ar
+            )
+        )
         finish(r.mr, r.lr, r.ar, r.mixr)
         loads[1].wait()
         mlp_start("r", 0, nn(r.mixr[...], r.wp[0]))
@@ -696,7 +725,7 @@
         for copy in swaps:
             copy.start()
         inp = r.inp[...].astype(F32)
-        gate = jax.nn.sigmoid(jnp.sum(inp * r.router[...], axis=-1, keepdims=True))
+        gate = jax.nn.sigmoid(jnp.sum(inp * r.router[...].reshape(1, D), axis=-1, keepdims=True))
         for load in loads[4:]:
             load.wait()
         for copy in swaps:
@@ -711,11 +740,13 @@
         r.nd[...] = normed
         r.kva[s, :, 0:W] = nn(normed, r.wq[1, 1]).astype(BF)
         r.kva[s, :, W : 2 * W] = nn(normed, r.wq[1, 2]).astype(BF)
-        r.qa[s] = nn(normed, r.wq[1, 0]).astype(BF)
-        spread = gather([(r.kva, r.kv_s, r.kv_r, True), (r.qa, r.q_s, r.q_r, False)])
-        spread.start()
-        spread.level()
-        spread.rest()
+        keys_all = gather(r.kva, r.kv_s, r.kv_r, True)
+        keys_all.start()
+        r.qa[s] = (nn(normed, r.wq[1, 0]).astype(BF) * SCALE).astype(BF)
+        query_all = gather(r.qa, r.q_s, r.q_r, False)
+        query_all.start()
+        keys_all.level()
+        query_all.level()
 
         def level_rows(ref, first=0):
             def get(ci, h):
@@ -736,19 +767,23 @@
         def dense_mask_back(ci):
             return (seg_line(ci).astype(F32) == r.segc[...]) & (own_pos <= far_pos + ci * CH)
 
-        attend(
-            z + 1,
-            lambda i: z - i,
-            lambda h: r.qa[s, :, head(h)],
-            level_rows(r.kva, 0),
-            level_rows(r.kva, H),
-            dense_mask,
-            r.md,
-            r.ld,
-            r.ad,
+        attend_start(r.md, r.ld, r.ad)
+        walk(
+            [keys_all],
+            lambda dz: attend(
+                z - dz,
+                lambda h: r.qa[s, :, head(h)],
+                level_rows(r.kva),
+                level_rows(r.kva, H),
+                dense_mask,
+                r.md,
+                r.ld,
+                r.ad,
+            ),
         )
         finish(r.md, r.ld, r.ad, r.mixd)
         mlp_start("d", 0, nn(r.mixd[...], r.wp[1]))
+        loop(1, query_all.last + 1, query_all.z_step)
         for x, w in chunks(F):
             r.dact[:, x : x + w] = nt(r.cot[...], r.wd[1, x : x + w, :])
         attn = mlp_total("d", 0)
@@ -765,6 +800,7 @@
 
         sum_start("down", r.cot, r.actd)
         sum_start("up", r.n2d, r.dpre)
+        loop(1, query_all.last + 1, query_all.y_step)
         dn, dg = rms_back(mlp_total("d", 1), r.hid[...], r.gains[1, 1:2])
         r.small[1:2] = dg
         dhid = r.cot[...].astype(F32) + dn
@@ -772,39 +808,53 @@
         r.dattn[...] = dhid.astype(BF)
         r.da[s] = nt(r.dattn[...], r.wp[1]).astype(BF)
         r.sta[s] = row_stats(lambda h: r.da[s, :, head(h)], r.md, r.ld, r.ad)
-        spread_back = gather([(r.da, r.da_s, r.da_r, False), (r.sta, r.st_s, r.st_r, False)])
-        spread_back.start()
-        spread_back.level()
-        back_query(
+        grad_all = gather(r.da, r.da_s, r.da_r, False)
+        stat_all = gather(r.sta, r.st_s, r.st_r, False)
+        for item in (grad_all, stat_all):
+            item.start()
+        for item in (grad_all, stat_all):
+            item.level()
+        query_all.level_end()
+        loop(1, query_all.last + 1, query_all.sib_step)
+        dq_d[...] = jnp.zeros((H, T, HD), F32)
+        dk_d[...] = jnp.zeros((H, T, HD), F32)
+        dv_d[...] = jnp.zeros((H, T, HD), F32)
+        loop(
+            0,
             z + 1,
-            lambda i: z - i,
-            lambda h: r.qa[s, :, head(h)],
-            lambda h: r.da[s, :, head(h)],
-            level_rows(r.kva, 0),
-            level_rows(r.kva, H),
-            dense_mask,
-            r.md,
-            r.ld,
-            dq_d,
+            lambda dz: back_query(
+                z - dz,
+                lambda h: r.qa[s, :, head(h)],
+                lambda h: r.da[s, :, head(h)],
+                level_rows(r.kva),
+                level_rows(r.kva, H),
+                dense_mask,
+                r.md,
+                r.ld,
+                dq_d,
+            ),
         )
-        spread_back.rest()
-        back_keys(
-            Z - z,
-            lambda i: z + i,
-            lambda h: r.kva[s, :, head(h)],
-            lambda h: r.kva[s, :, head(H + h)],
-            level_rows(r.qa),
-            level_rows(r.da),
-            dense_mask_back,
-            lambda ci, line: level_line(r.sta, line)(ci),
-            dk_d,
-            dv_d,
+        sum_y("down")
+        walk(
+            [grad_all, stat_all],
+            lambda dz: back_keys(
+                z + dz,
+                lambda h: r.kva[s, :, head(h)],
+                lambda h: r.kva[s, :, head(H + h)],
+                level_rows(r.qa),
+                level_rows(r.da),
+                dense_mask_back,
+                lambda ci, line: level_line(r.sta, line)(ci),
+                dk_d,
+                dv_d,
+            ),
         )
+        sum_y("up")
         pack_grads(dq_d, dk_d, dv_d, r.g3)
         mlp_start("d", 3, front_back(r.g3, 1))
+        sum_start("qkv", r.nd, r.g3)
         sum_start("proj", r.dattn, r.mixd)
-        sum_start("qkv", r.nd, r.g3)
-        sum_y("down")
+        sum_z("down")
         dn, dg = rms_back(mlp_total("d", 3), r.ro[...], r.gains[1, 0:1])
         r.small[0:1] = dg
         dro = r.dro[...] + dn
@@ -812,10 +862,11 @@
 
         sel = r.sel[...].astype(F32)
         inp = r.inp[...].astype(F32)
-        gate = jax.nn.sigmoid(jnp.sum(inp * r.router[...], axis=-1, keepdims=True))
+        gate = jax.nn.sigmoid(jnp.sum(inp * r.router[...].reshape(1, D), axis=-1, keepdims=True))
         dlogit = jnp.sum(dro * sel, axis=-1, keepdims=True) * gate * (1.0 - gate)
         scatter_rows((gate * dro).astype(BF))
-        spread_rows()
+        spread_start()
+        spread_end(lambda: None)
         r.small[2:3] = jnp.sum(inp * dlogit, axis=0, keepdims=True)
         r.small[3:8] = jnp.zeros((5, D), F32)
         r.sblk[...] = jnp.zeros((S, 8, 128), F32)
@@ -829,6 +880,8 @@
 
         lax.fori_loop(1, S, send_small, 0)
         r.srec[s] = r.sblk[s]
+        sum_y("qkv")
+        sum_y("proj")
 
         dmlp = r.rows[half, :]
         r.attr[...] = r.attr[...] + r.chh[...].astype(F32)
@@ -847,39 +900,44 @@
         for copy in swaps:
             copy.start()
         routed_start("proj", r.dattr[...], r.mixr[...])
-        back_query(
-            GN,
-            routed_pick,
-            half_rows(r.qr),
-            lambda h: r.dor[gi, :, head(h)],
-            part_rows(r.kr),
-            part_rows(r.vr),
-            routed_mask,
-            r.mr,
-            r.lr,
-            dq_r,
+        sum_z("up")
+        dq_r[...] = jnp.zeros((H, RH, HD), F32)
+        dk_r[...] = jnp.zeros((H, RH, HD), F32)
+        dv_r[...] = jnp.zeros((H, RH, HD), F32)
+        routed_loop(
+            lambda ci: back_query(
+                ci,
+                half_rows(r.qr),
+                lambda h: r.dor[gi, :, head(h)],
+                part_rows(r.kr),
+                part_rows(r.vr),
+                routed_mask,
+                r.mr,
+                r.lr,
+                dq_r,
+            )
         )
         for copy in swaps:
             copy.wait()
-        back_keys(
-            GN,
-            routed_pick,
-            half_rows(r.kr),
-            half_rows(r.vr),
-            part_rows(r.qr),
-            lambda ci, h: r.dor[ci, :, head(h)],
-            routed_mask_back,
-            lambda ci, line: r.str[ci][line : line + 1],
-            dk_r,
-            dv_r,
+        routed_loop(
+            lambda ci: back_keys(
+                ci,
+                half_rows(r.kr),
+                half_rows(r.vr),
+                part_rows(r.qr),
+                lambda ci, h: r.dor[pl.ds(ci * 2, 2), :, head(h)].reshape(2 * RH, HD),
+                routed_mask_back,
+                lambda ci, line: jnp.concatenate([r.str[ci * 2 + j][line : line + 1] for j in range(2)], axis=1),
+                dk_r,
+                dv_r,
+            )
         )
         pack_grads(dq_r, dk_r, dv_r, r.g3r)
         mlp_start("r", 3, front_back(r.g3r, 0))
         routed_start("qkv", r.nr[...], r.g3r[...])
-        sum_y("up")
-        sum_y("proj")
-        sum_y("qkv")
-        sum_z("down")
+        sum_end("down")
+        sum_z("qkv")
+        sum_z("proj")
         dn, dg1 = rms_back(mlp_total("r", 3), r.chh[...].astype(F32), r.gains[0, 0:1])
         r.chg[gi] = (r.attr[...] + dn).astype(BF)
         r.gr[gi] = jnp.concatenate([dg1, dg2, jnp.zeros((6, D), F32)], axis=0)
@@ -891,22 +949,45 @@
         r.rg_o[...] = jnp.sum(r.gr[...], axis=0)[0:2]
         back = nn(r.oht[...], r.chg[...].reshape(R, D))
         inp = r.inp[...].astype(F32)
-        gate = jax.nn.sigmoid(jnp.sum(inp * r.router[...], axis=-1, keepdims=True))
+        gate = jax.nn.sigmoid(jnp.sum(inp * r.router[...].reshape(1, D), axis=-1, keepdims=True))
         dlogit = jnp.sum(r.dro[...] * r.sel[...].astype(F32), axis=-1, keepdims=True) * gate * (1.0 - gate)
-        r.gi_o[...] = r.dro[...] + back + dlogit * r.router[...]
+        r.gi_o[...] = r.dro[...] + back + dlogit * r.router[...].reshape(1, D)
 
         r.do_o[...] = (r.hid[...] + mlp_total("d", 2)).astype(BF)
         some = pl.ds(0, S - 1)
         remote(r.sblk.at[some], r.srec.at[some], r.sm_s.at[0], r.sm_s.at[1], s, m).wait()
         r.sm_o[...] = jnp.sum(r.srec[...], axis=0)
-        for k in ("up", "proj", "qkv"):
-            sum_z(k)
         for k in KINDS:
             routed_end(k)
-        for k in KINDS:
+        for k in ("up", "qkv", "proj"):
             sum_end(k)
-        spread.end()
-        spread_back.end()
+        for item in (keys_all, query_all, grad_all, stat_all):
+            item.end()
+
+    def layout(*refs):
+        moved = [refs[i] for i in (0, 1, 2, 5, 6, 7, 8)]
+        sm, rg = refs[3:5]
+        moved_o = [refs[9 + i] for i in (0, 1, 2, 5, 6, 7, 8)]
+        gains_o, router_o = refs[12:14]
+        held, sems = refs[18:25], refs[25]
+        ways = [
+            (pltpu.make_async_copy(a, v, sems.at[0, i]), pltpu.make_async_copy(v, b, sems.at[1, i]))
+            for i, (a, v, b) in enumerate(zip(moved, held, moved_o))
+        ]
+        for into, _ in ways:
+            into.start()
+        s = lax.axis_index("seq")
+        routed = rg[:, 0:DR]
+        for p in range(1, S):
+            routed = jnp.where(s == p, rg[:, p * DR : (p + 1) * DR], routed)
+        gains_o[0] = routed
+        gains_o[1] = sm[0:2, 0:DR]
+        router_o[...] = sm[2:3, 0:DR]
+        for into, out in ways:
+            into.wait()
+            out.start()
+        for _, out in ways:
+            out.wait()
 
     def run(inp, segments, picks, gains, router, qkv, proj, up, down, cot):
         args = (
@@ -914,7 +995,7 @@
             segments.reshape(1, T),
             picks,
             gains,
-            router.reshape(1, D),
+            router,
             cot,
             jnp.asarray(target),
             qkv,
@@ -935,11 +1016,29 @@
             ),
             name="train_step",
         )(*args)
-        ro, do, gi, sm, rg, gq, gp, gu, gd = res
-        at = lax.axis_index("seq") * DR
-        routed_gains = lax.dynamic_slice_in_dim(rg, at, DR, 1)
-        gains_grad = jnp.stack([routed_gains, sm[0:2, 0:DR]])
-        return (ro, do, gi, gains_grad, sm[2, 0:DR], gq, gp, gu, gd)
+        shapes = [
+            ((T, D), BF),
+            ((T, D), BF),
+            ((T, D), F32),
+            ((2, 2, DR), F32),
+            ((1, DR), F32),
+            ((2, 3, DR, W), F32),
+            ((2, DR, W), F32),
+            ((2, DR, F), F32),
+            ((2, DR, F), F32),
+        ]
+        last = pl.pallas_call(
+            layout,
+            out_shape=[jax.ShapeDtypeStruct(sh, dt) for sh, dt in shapes],
+            in_specs=[hbm] * 3 + [vmem] * 2 + [hbm] * 4,
+            out_specs=[hbm] * 3 + [vmem] * 2 + [hbm] * 4,
+            scratch_shapes=[pltpu.VMEM(*shapes[i]) for i in (0, 1, 2, 5, 6, 7, 8)] + [DMA((2, 7))],
+            compiler_params=pltpu.CompilerParams(vmem_limit_bytes=62 * 1024 * 1024),
+            name="layout",
+        )(*res)
+        ro, do, gi, gains_grad, router_grad, gq, gp, gu, gd = last
+        gp, gd = jnp.swapaxes(gp, 1, 2), jnp.swapaxes(gd, 1, 2)
+        return (ro, do, gi, gains_grad, router_grad.reshape(DR), gq, gp, gu, gd)
 
     return run
 

time: 226 us -> 183 us (0.81)
  Pallas kernels: 212 us -> 182 us
  local copies, waits for them, and re-layouts: 13.3 us -> 0 us
    pallas_call x1, Pallas kernels: 212 us -> 178 us  [run(): pl.pallas_call(kernel, out_shape=[jax.ShapeDtypeStruct(sh, dt) for sh, dt...]
    unnamed x13 -> x0, local copies, waits for them, and re-layouts: 10 us -> none
    pallas_call x0 -> x1, Pallas kernels: none -> 3.98 us  [run(): pl.pallas_call(layout, out_shape=[jax.ShapeDtypeStruct(sh, dt) for sh, dt...]
where the time goes in v2:
time: 183 us
  Pallas kernels  182 us (99%)
    pallas_call x1, Pallas kernels, run(): pl.pallas_call(kernel, out_shape=[jax.ShapeDtypeStruct(sh, dt) for sh, dt...  178 us
    pallas_call x1, Pallas kernels, run(): pl.pallas_call(layout, out_shape=[jax.ShapeDtypeStruct(sh, dt) for sh, dt...  3.98 us

profile of v2, /device:TPU:0, one launch (start us, length us, event | category | flops | bytes accessed | tf_op | source)
XLA Modules:
  0.0 182.8 jit_solution(10074611061556224100)
XLA Ops:
  0.6 178.0 %train_step.1 = (bf16[128,768]{1,0:T(8,128)(2,1)}, bf16[128,768]{1,0:T(8,128)(2,1)}, f32[128,768]{1,0:T(8,128)}, f32[8,128]{1,0:T(8,128)}, f32[2,768]{1,0:T(2,12...) custom-call(bf16[128,768]{1,0:T(8,128)(2,1)} %refs_0_.1, ...), custom_call_target="tpu_custom_call" | custom-call | tf_op jit(solution)/shard_map/train_step/pallas_call | solution.py:1008
  178.7 4.0 %layout.1 = (bf16[128,768]{1,0:T(8,128)(2,1)}, bf16[128,768]{1,0:T(8,128)(2,1)}, f32[128,768]{1,0:T(8,128)}, f32[2,2,48]{2,1,0:T(2,128)}, f32[1,48]{1,0:T(1,128)...) custom-call(bf16[128,768]{1,0:T(8,128)(2,1)} %get-tuple-element.27.refs_0, ...), custom_call_target="tpu_custom_call" | custom-call | tf_op jit(solution)/shard_map/layout/pallas_call | solution.py:1030

commit v3 on v2

--- a/solution.py
+++ b/solution.py
@@ -85,15 +85,16 @@
     DM = D // n
     DR = D // S
     DRP = -(-DR // 16) * 16
-    Q = ZY * DRP
+    ZD = Z * DRP
+    QY = 2 * ZD
     XW = {"down": F, "up": F, "proj": W, "qkv": 3 * W}
 
-    target = np.full((2, 1, Q), -1, np.int32)
-    for core in range(2):
-        for yy in range(Y):
+    target = np.full((Y, 1, QY), -1, np.int32)
+    for yy in range(Y):
+        for core in range(2):
             for zz in range(Z):
                 for j in range(DR):
-                    target[core, 0, (yy * Z + zz) * DRP + j] = ((zz * Y + yy) * 2 + core) * DR + j
+                    target[yy, 0, (core * Z + zz) * DRP + j] = ((zz * Y + yy) * 2 + core) * DR + j
 
     ins = ["inp", "segr", "picks", "gains", "router", "cot", "target", "qkv_h", "proj_h", "up_h", "down_h"]
     outs = {
@@ -150,17 +151,13 @@
         "md": ((H, T, 1), F32),
         "ld": ((H, T, 1), F32),
         "ad": ((H, T, HD), F32),
-        "mixd": ((T, W), BF),
         "hid": ((T, D), F32),
         "n2d": ((T, D), BF),
         "dact": ((T, F), F32),
-        "actd": ((T, F), BF),
-        "dpre": ((T, F), BF),
         "dattn": ((T, D), BF),
         "dq": ((H, max(T, RH), HD), F32),
         "dk": ((H, max(T, RH), HD), F32),
         "dv": ((H, max(T, RH), HD), F32),
-        "g3": ((T, 3 * W), BF),
         "dro": ((T, D), F32),
         "small": ((8, D), F32),
         "sblk": ((S, 8, 128), F32),
@@ -171,14 +168,15 @@
         "dattr": ((RH, D), BF),
         "g3r": ((RH, 3 * W), BF),
         "gr": ((GN, 8, D), F32),
-        "sele": ((2, D, Q), BF),
+        "sele": ((Y, D, QY), BF),
     }
     for k in KINDS:
         X = XW[k]
-        vm["keep_" + k] = ((Y, Z, DRP, X), F32)
-        vm["send_" + k] = ((Y, Z, DRP, X), BF)
-        vm["sibr_" + k] = ((Y, Z, DRP, X), BF)
-        vm["yrec_" + k] = ((Y - 1, Z, DRP, X), BF)
+        vm["left_" + k] = ((LEVEL, T, QY), BF)
+        vm["away_" + k] = ((Y - 1, T, QY), BF)
+        vm["right_" + k] = ((LEVEL, T, X), BF)
+        vm["zsend_" + k] = ((Z, DRP, X), BF)
+        vm["zown_" + k] = ((DRP, X), F32)
         vm["zrec_" + k] = ((Z - 1, DRP, X), BF)
         vm["rsend_" + k] = ((GN - 1, DRP, X), BF)
         vm["rkeep_" + k] = ((DRP, X), F32)
@@ -203,10 +201,8 @@
         "st_s": (n_sends,),
         "st_r": (S,),
         "sm_s": (2,),
-        "gs_s": (4,),
-        "gs_r": (4,),
-        "gy_s": (4, Y - 1),
-        "gy_r": (4, Y - 1),
+        "gl_s": (4, 2, 2 * Y - 1),
+        "gl_r": (4, 2, LEVEL),
         "gz_s": (4, Z - 1),
         "gz_r": (4, Z - 1),
     }
@@ -542,29 +538,57 @@
 
             loop(1, last + 1, step)
 
-        def sum_start(k, lhs, rhs):
+        lev = lax.rem(s, LEVEL)
+
+        def level_slot(dy, cc):
+            return lax.rem(y + dy, Y) * 2 + cc
+
+        def level_copy(k, side, j, src, slot, dst):
             i = KINDS.index(k)
-            out = nn(lhs[...], r.sele[1 - c]).astype(BF)
-            stay = nn(lhs[...], r.sele[c]).astype(BF)
-            for x, w in chunks(XW[k]):
-                g["send_" + k][:, :, :, x : x + w] = tn(out, rhs[:, x : x + w]).astype(BF).reshape(Y, Z, DRP, w)
-            remote(g["send_" + k], g["sibr_" + k], r.gs_s.at[i], r.gs_r.at[i], sib, m).start()
-            for x, w in chunks(XW[k]):
-                g["keep_" + k][:, :, :, x : x + w] = tn(stay, rhs[:, x : x + w]).reshape(Y, Z, DRP, w)
-
-        def y_copy(k, i, dy):
+            buf = g[("left_", "right_")[side] + k]
+            return remote(src, buf.at[slot], r.gl_s.at[i, side, j], r.gl_r.at[i, side, slot], dst, m)
+
+        def own_copies(k, side):
+            mine = g[("left_", "right_")[side] + k].at[lev]
+            out = [level_copy(k, side, 0, mine, lev, sib)]
+            for dy in range(1, Y):
+                src = g["away_" + k].at[dy - 1] if side == 0 else mine
+                out.append(level_copy(k, side, dy, src, lev, rank(z, lax.rem(y + dy, Y), c)))
+            return out
+
+        def far_copies(k):
+            return [
+                level_copy(k, side, Y + dy - 1, g[("left_", "right_")[side] + k].at[level_slot(dy, c)], level_slot(dy, c), sib)
+                for side in range(2)
+                for dy in range(1, Y)
+            ]
+
+        def level_wait(k, slot):
+            for side in range(2):
+                buf = g[("left_", "right_")[side] + k]
+                level_copy(k, side, 0, buf.at[slot], slot, sib).wait_recv()
+
+        def sum_left(k, lhs):
+            g["left_" + k][lev] = nn(lhs[...], r.sele[y]).astype(BF)
+            for dy in range(1, Y):
+                g["away_" + k][dy - 1] = nn(lhs[...], r.sele[lax.rem(y + dy, Y)]).astype(BF)
+            for copy in own_copies(k, 0):
+                copy.start()
+
+        def sum_right(k):
+            for copy in own_copies(k, 1):
+                copy.start()
+
+        def sum_far(k):
+            for dy in range(1, Y):
+                level_wait(k, level_slot(dy, c))
+            for copy in far_copies(k):
+                copy.start()
+
+        def z_copy(k, dz):
+            i = KINDS.index(k)
             return remote(
-                g["sibr_" + k].at[lax.rem(y + dy, Y)],
-                g["yrec_" + k].at[dy - 1],
-                r.gy_s.at[i, dy - 1],
-                r.gy_r.at[i, dy - 1],
-                rank(z, lax.rem(y + dy, Y), c),
-                m,
-            )
-
-        def z_copy(k, i, dz):
-            return remote(
-                g["yrec_" + k].at[0, lax.rem(z + dz, Z)],
+                g["zsend_" + k].at[lax.rem(z + dz, Z)],
                 g["zrec_" + k].at[dz - 1],
                 r.gz_s.at[i, dz - 1],
                 r.gz_r.at[i, dz - 1],
@@ -572,30 +596,20 @@
                 m,
             )
 
-        def sum_y(k):
-            i = KINDS.index(k)
-            remote(g["send_" + k], g["sibr_" + k], r.gs_s.at[i], r.gs_r.at[i], sib, m).wait()
-            for dy in range(1, Y):
-                yy = lax.rem(y + dy, Y)
-                g["sibr_" + k][yy] = (g["keep_" + k][yy] + g["sibr_" + k][yy].astype(F32)).astype(BF)
-                y_copy(k, i, dy).start()
-
         def sum_z(k):
-            i = KINDS.index(k)
-            for dy in range(1, Y):
-                y_copy(k, i, dy).wait()
-
-            def total(zz):
-                t = g["keep_" + k][y, zz] + g["sibr_" + k][y, zz].astype(F32)
-                for dy in range(1, Y):
-                    t = t + g["yrec_" + k][dy - 1, zz].astype(F32)
-                return t
-
+            for dy in range(Y):
+                level_wait(k, level_slot(dy, 1 - c))
+            left = g["left_" + k][...].reshape(LEVEL * T, QY)
+            left = jnp.where(c == 0, left[:, 0:ZD], left[:, ZD:QY])
+            for x, w in chunks(XW[k]):
+                total = tn(left, g["right_" + k][:, :, x : x + w].reshape(LEVEL * T, w)).reshape(Z, DRP, w)
+                g["zsend_" + k][:, :, x : x + w] = total.astype(BF)
+                own = total[0]
+                for zz in range(1, Z):
+                    own = jnp.where(z == zz, total[zz], own)
+                g["zown_" + k][:, x : x + w] = own
             for dz in range(1, Z):
-                zz = lax.rem(z + dz, Z)
-                g["yrec_" + k][0, zz] = total(zz).astype(BF)
-                z_copy(k, i, dz).start()
-            g["keep_" + k][y, z] = total(z)
+                z_copy(k, dz).start()
 
         def put(b, k, value):
             if k == "qkv":
@@ -605,12 +619,18 @@
                 g[k + "_o"][b] = value[0:DR]
 
         def sum_end(k):
-            i = KINDS.index(k)
-            t = g["keep_" + k][y, z]
+            t = g["zown_" + k][...]
             for dz in range(1, Z):
-                z_copy(k, i, dz).wait()
+                z_copy(k, dz).wait()
                 t = t + g["zrec_" + k][dz - 1].astype(F32)
             put(1, k, t)
+
+        def sum_sent(k):
+            for side in range(2):
+                for copy in own_copies(k, side):
+                    copy.wait_send()
+            for copy in far_copies(k):
+                copy.wait_send()
 
         def routed_copy(k, j):
             i = 6 + KINDS.index(k)
@@ -651,9 +671,9 @@
         mine = r.posr[gi // 2][0:1]
         r.posc[...] = column(jnp.where(lax.rem(gi, 2) == 0, mine[:, 0:RH], mine[:, RH : 2 * RH]))
         r.segc[...] = column(r.segr[...])
-        for par in range(2):
-            ids = lax.broadcasted_iota(jnp.int32, (D, Q), 0)
-            r.sele[par] = jnp.where(ids == r.target[par], 1.0, 0.0).astype(BF)
+        for yy in range(Y):
+            ids = lax.broadcasted_iota(jnp.int32, (D, QY), 0)
+            r.sele[yy] = jnp.where(ids == r.target[yy], 1.0, 0.0).astype(BF)
         spread_end(lambda: lax.fori_loop(1, S, send_segments, 0))
         some = pl.ds(0, S - 1)
         remote(r.sega.at[some], r.sega.at[some], r.seg_s.at[0], r.seg_s.at[1], s, m).wait()
@@ -708,6 +728,7 @@
         finish(r.mr, r.lr, r.ar, r.mixr)
         loads[1].wait()
         mlp_start("r", 0, nn(r.mixr[...], r.wp[0]))
+        sum_left("down", r.cot)
         loads[2].wait()
         loads[3].wait()
         attn = mlp_total("r", 0)
@@ -781,9 +802,10 @@
                 r.ad,
             ),
         )
-        finish(r.md, r.ld, r.ad, r.mixd)
-        mlp_start("d", 0, nn(r.mixd[...], r.wp[1]))
+        finish(r.md, r.ld, r.ad, r.right_proj.at[lev])
+        mlp_start("d", 0, nn(r.right_proj[lev], r.wp[1]))
         loop(1, query_all.last + 1, query_all.z_step)
+        sum_left("qkv", r.nd)
         for x, w in chunks(F):
             r.dact[:, x : x + w] = nt(r.cot[...], r.wd[1, x : x + w, :])
         attn = mlp_total("d", 0)
@@ -793,13 +815,13 @@
         r.n2d[...] = normed
         for x, w in chunks(F):
             active, slope = gelu_pair(nn(normed, r.wu[1, :, x : x + w]))
-            r.actd[:, x : x + w] = active.astype(BF)
-            r.dpre[:, x : x + w] = (r.dact[:, x : x + w] * slope).astype(BF)
-        mlp_start("d", 1, nt(r.dpre[...], r.wu[1]))
-        mlp_start("d", 2, nn(r.actd[...], r.wd[1]))
-
-        sum_start("down", r.cot, r.actd)
-        sum_start("up", r.n2d, r.dpre)
+            r.right_down[lev, :, x : x + w] = active.astype(BF)
+            r.right_up[lev, :, x : x + w] = (r.dact[:, x : x + w] * slope).astype(BF)
+        sum_right("down")
+        mlp_start("d", 1, nt(r.right_up[lev], r.wu[1]))
+        mlp_start("d", 2, nn(r.right_down[lev], r.wd[1]))
+
+        sum_left("up", r.n2d)
         loop(1, query_all.last + 1, query_all.y_step)
         dn, dg = rms_back(mlp_total("d", 1), r.hid[...], r.gains[1, 1:2])
         r.small[1:2] = dg
@@ -814,6 +836,7 @@
             item.start()
         for item in (grad_all, stat_all):
             item.level()
+        sum_right("up")
         query_all.level_end()
         loop(1, query_all.last + 1, query_all.sib_step)
         dq_d[...] = jnp.zeros((H, T, HD), F32)
@@ -834,7 +857,6 @@
                 dq_d,
             ),
         )
-        sum_y("down")
         walk(
             [grad_all, stat_all],
             lambda dz: back_keys(
@@ -849,12 +871,14 @@
                 dv_d,
             ),
         )
-        sum_y("up")
-        pack_grads(dq_d, dk_d, dv_d, r.g3)
-        mlp_start("d", 3, front_back(r.g3, 1))
-        sum_start("qkv", r.nd, r.g3)
-        sum_start("proj", r.dattn, r.mixd)
+        sum_far("down")
+        sum_far("up")
         sum_z("down")
+        pack_grads(dq_d, dk_d, dv_d, r.right_qkv.at[lev])
+        mlp_start("d", 3, front_back(r.right_qkv.at[lev], 1))
+        sum_left("proj", r.dattn)
+        sum_right("qkv")
+        sum_right("proj")
         dn, dg = rms_back(mlp_total("d", 3), r.ro[...], r.gains[1, 0:1])
         r.small[0:1] = dg
         dro = r.dro[...] + dn
@@ -880,8 +904,9 @@
 
         lax.fori_loop(1, S, send_small, 0)
         r.srec[s] = r.sblk[s]
-        sum_y("qkv")
-        sum_y("proj")
+        sum_z("up")
+        sum_far("qkv")
+        sum_far("proj")
 
         dmlp = r.rows[half, :]
         r.attr[...] = r.attr[...] + r.chh[...].astype(F32)
@@ -900,7 +925,8 @@
         for copy in swaps:
             copy.start()
         routed_start("proj", r.dattr[...], r.mixr[...])
-        sum_z("up")
+        sum_z("qkv")
+        sum_z("proj")
         dq_r[...] = jnp.zeros((H, RH, HD), F32)
         dk_r[...] = jnp.zeros((H, RH, HD), F32)
         dv_r[...] = jnp.zeros((H, RH, HD), F32)
@@ -936,8 +962,7 @@
         mlp_start("r", 3, front_back(r.g3r, 0))
         routed_start("qkv", r.nr[...], r.g3r[...])
         sum_end("down")
-        sum_z("qkv")
-        sum_z("proj")
+        sum_end("up")
         dn, dg1 = rms_back(mlp_total("r", 3), r.chh[...].astype(F32), r.gains[0, 0:1])
         r.chg[gi] = (r.attr[...] + dn).astype(BF)
         r.gr[gi] = jnp.concatenate([dg1, dg2, jnp.zeros((6, D), F32)], axis=0)
@@ -959,10 +984,12 @@
         r.sm_o[...] = jnp.sum(r.srec[...], axis=0)
         for k in KINDS:
             routed_end(k)
-        for k in ("up", "qkv", "proj"):
-            sum_end(k)
+        sum_end("qkv")
+        sum_end("proj")
         for item in (keys_all, query_all, grad_all, stat_all):
             item.end()
+        for k in KINDS:
+            sum_sent(k)
 
     def layout(*refs):
         moved = [refs[i] for i in (0, 1, 2, 5, 6, 7, 8)]

time: 183 us -> 171 us (0.934)
  Pallas kernels: 182 us -> 170 us
    pallas_call x1, Pallas kernels: 178 us -> 166 us  [run(): pl.pallas_call(kernel, out_shape=[jax.ShapeDtypeStruct(sh, dt) for sh, dt...]
where the time goes in v3:
time: 171 us
  Pallas kernels  170 us (99%)
    pallas_call x1, Pallas kernels, run(): pl.pallas_call(kernel, out_shape=[jax.ShapeDtypeStruct(sh, dt) for sh, dt...  166 us
    pallas_call x1, Pallas kernels, run(): pl.pallas_call(layout, out_shape=[jax.ShapeDtypeStruct(sh, dt) for sh, dt...  3.98 us

profile of v3, /device:TPU:0, one launch (start us, length us, event | category | flops | bytes accessed | tf_op | source)
XLA Modules:
  0.0 170.7 jit_solution(7132442193109611254)
XLA Ops:
  0.6 165.9 %train_step.1 = (bf16[128,768]{1,0:T(8,128)(2,1)}, bf16[128,768]{1,0:T(8,128)(2,1)}, f32[128,768]{1,0:T(8,128)}, f32[8,128]{1,0:T(8,128)}, f32[2,768]{1,0:T(2,12...) custom-call(bf16[128,768]{1,0:T(8,128)(2,1)} %refs_0_.1, ...), custom_call_target="tpu_custom_call" | custom-call | tf_op jit(solution)/shard_map/train_step/pallas_call | solution.py:1035
  166.5 4.0 %layout.1 = (bf16[128,768]{1,0:T(8,128)(2,1)}, bf16[128,768]{1,0:T(8,128)(2,1)}, f32[128,768]{1,0:T(8,128)}, f32[2,2,48]{2,1,0:T(2,128)}, f32[1,48]{1,0:T(1,128)...) custom-call(bf16[128,768]{1,0:T(8,128)(2,1)} %get-tuple-element.27.refs_0, ...), custom_call_target="tpu_custom_call" | custom-call | tf_op jit(solution)/shard_map/layout/pallas_call | solution.py:1057

commit v4 on v3

--- a/solution.py
+++ b/solution.py
@@ -20,6 +20,8 @@
 GELU_A = 0.044715
 GELU_B = float(np.sqrt(2.0 / np.pi))
 WIDE = 1536
+KV_CHAIN = True
+DO_CHAIN = False
 KINDS = ("down", "up", "proj", "qkv")
 
 
@@ -87,6 +89,7 @@
     DRP = -(-DR // 16) * 16
     ZD = Z * DRP
     QY = 2 * ZD
+    FOLDED = KINDS if Z == 4 else ()
     XW = {"down": F, "up": F, "proj": W, "qkv": 3 * W}
 
     target = np.full((Y, 1, QY), -1, np.int32)
@@ -177,7 +180,8 @@
         vm["right_" + k] = ((LEVEL, T, X), BF)
         vm["zsend_" + k] = ((Z, DRP, X), BF)
         vm["zown_" + k] = ((DRP, X), F32)
-        vm["zrec_" + k] = ((Z - 1, DRP, X), BF)
+        vm["zrec_" + k] = ((Z, DRP, X), BF)
+        vm["zfar_" + k] = ((DRP, X), BF)
         vm["rsend_" + k] = ((GN - 1, DRP, X), BF)
         vm["rkeep_" + k] = ((DRP, X), F32)
         vm["rrec_" + k] = ((GN - 1, DRP, X), BF)
@@ -434,7 +438,7 @@
 
             lax.fori_loop(low, high, step, 0)
 
-        def gather(buf, ss, rs, up):
+        def gather(buf, ss, rs, up, chain):
             sign = -1 if up else 1
             last = z if up else Z - 1 - z
             ahead = Z - 1 - z if up else z
@@ -452,7 +456,10 @@
                 return lax.rem(y + dy, Y)
 
             def copies(each):
-                loop(1, ahead + 1, lambda dz: each(copy(s, rank(z - sign * dz, y, c), dz - 1)))
+                if chain:
+                    pl.when(ahead > 0)(lambda: each(copy(s, rank(z - sign, y, c), 0)))
+                else:
+                    loop(1, ahead + 1, lambda dz: each(copy(s, rank(z - sign * dz, y, c), dz - 1)))
                 for dy in range(1, Y):
                     each(copy(s, rank(z, side(dy), c), at_y + dy - 1))
                 each(copy(s, sib, at_sib))
@@ -481,8 +488,14 @@
                 for dy in range(Y):
                     recv(rank(z, side(dy), 1 - c))
 
+            def onward(dz, each):
+                if chain:
+                    slot = rank(z + sign * dz, y, c)
+                    pl.when(ahead > 0)(lambda: each(copy(slot, rank(z - sign, y, c), dz)))
+
             def z_step(dz):
                 recv(rank(z + sign * dz, y, c))
+                onward(dz, lambda one: one.start())
                 for one in z_copies(dz):
                     one.start()
 
@@ -501,6 +514,7 @@
                     level_copy(dy).wait_send()
 
                 def sent(dz):
+                    onward(dz, lambda one: one.wait_send())
                     for one in z_copies(dz):
                         one.wait_send()
                     for dy in range(1, Y):
@@ -608,8 +622,81 @@
                 for zz in range(1, Z):
                     own = jnp.where(z == zz, total[zz], own)
                 g["zown_" + k][:, x : x + w] = own
-            for dz in range(1, Z):
-                z_copy(k, dz).start()
+            if k in FOLDED:
+                fold_first(k, lambda one: one.start())
+            else:
+                for dz in range(1, Z):
+                    z_copy(k, dz).start()
+
+        edge = (z == 0) | (z == Z - 1)
+        low_half = z < 2
+        near = jnp.where(low_half, jnp.where(z == 0, 1, 0), jnp.where(z == 3, 2, 3))
+        three = pl.ds(jnp.where(low_half, 1, 0), 3)
+
+        def fold_first(k, then):
+            i = KINDS.index(k)
+            one = pl.ds(near, 1)
+            for cond, blocks in ((edge, three), (jnp.logical_not(edge), one)):
+                pl.when(cond)(
+                    lambda blocks=blocks: then(
+                        remote(
+                            g["zsend_" + k].at[blocks],
+                            g["zrec_" + k].at[blocks],
+                            r.gz_s.at[i, 0],
+                            r.gz_r.at[i, 0],
+                            rank(near, y, c),
+                            m,
+                        )
+                    )
+                )
+
+        def fold_copies(k):
+            i = KINDS.index(k)
+            far = (3 - z, jnp.where(low_half, 3, 0))
+            return [
+                remote(
+                    g["zsend_" + k].at[b],
+                    g["zfar_" + k],
+                    r.gz_s.at[i, 1 + j],
+                    r.gz_r.at[i, 1],
+                    rank(b, y, c),
+                    m,
+                )
+                for j, b in enumerate(far)
+            ]
+
+        def fold_recv(k, blocks):
+            i = KINDS.index(k)
+            some = g["zrec_" + k].at[blocks]
+            remote(some, some, r.gz_s.at[i, 0], r.gz_r.at[i, 0], sib, m).wait_recv()
+
+        def sum_mid(k):
+            if k not in FOLDED:
+                return
+
+            def work():
+                fold_recv(k, three)
+                for b, copy in zip((3 - z, jnp.where(low_half, 3, 0)), fold_copies(k)):
+                    t = g["zsend_" + k][b].astype(F32) + g["zrec_" + k][b].astype(F32)
+                    g["zsend_" + k][b] = t.astype(BF)
+                    copy.start()
+
+            pl.when(jnp.logical_not(edge))(work)
+
+        def fold_end(k):
+            i = KINDS.index(k)
+            pl.when(edge)(lambda: fold_recv(k, pl.ds(z, 1)))
+            far = g["zfar_" + k]
+            remote(far, far, r.gz_s.at[i, 1], r.gz_r.at[i, 1], sib, m).wait_recv()
+            fold_first(k, lambda one: one.wait_send())
+
+            def sent():
+                for copy in fold_copies(k):
+                    copy.wait_send()
+
+            pl.when(jnp.logical_not(edge))(sent)
+            t = g["zown_" + k][...] + g["zrec_" + k][z].astype(F32) + far[...].astype(F32)
+            put(1, k, t)
 
         def put(b, k, value):
             if k == "qkv":
@@ -619,6 +706,8 @@
                 g[k + "_o"][b] = value[0:DR]
 
         def sum_end(k):
+            if k in FOLDED:
+                return fold_end(k)
             t = g["zown_" + k][...]
             for dz in range(1, Z):
                 z_copy(k, dz).wait()
@@ -761,10 +850,10 @@
         r.nd[...] = normed
         r.kva[s, :, 0:W] = nn(normed, r.wq[1, 1]).astype(BF)
         r.kva[s, :, W : 2 * W] = nn(normed, r.wq[1, 2]).astype(BF)
-        keys_all = gather(r.kva, r.kv_s, r.kv_r, True)
+        keys_all = gather(r.kva, r.kv_s, r.kv_r, True, KV_CHAIN)
         keys_all.start()
         r.qa[s] = (nn(normed, r.wq[1, 0]).astype(BF) * SCALE).astype(BF)
-        query_all = gather(r.qa, r.q_s, r.q_r, False)
+        query_all = gather(r.qa, r.q_s, r.q_r, False, False)
         query_all.start()
         keys_all.level()
         query_all.level()
@@ -830,8 +919,8 @@
         r.dattn[...] = dhid.astype(BF)
         r.da[s] = nt(r.dattn[...], r.wp[1]).astype(BF)
         r.sta[s] = row_stats(lambda h: r.da[s, :, head(h)], r.md, r.ld, r.ad)
-        grad_all = gather(r.da, r.da_s, r.da_r, False)
-        stat_all = gather(r.sta, r.st_s, r.st_r, False)
+        grad_all = gather(r.da, r.da_s, r.da_r, False, DO_CHAIN)
+        stat_all = gather(r.sta, r.st_s, r.st_r, False, DO_CHAIN)
         for item in (grad_all, stat_all):
             item.start()
         for item in (grad_all, stat_all):
@@ -890,21 +979,14 @@
         dlogit = jnp.sum(dro * sel, axis=-1, keepdims=True) * gate * (1.0 - gate)
         scatter_rows((gate * dro).astype(BF))
         spread_start()
-        spread_end(lambda: None)
         r.small[2:3] = jnp.sum(inp * dlogit, axis=0, keepdims=True)
-        r.small[3:8] = jnp.zeros((5, D), F32)
-        r.sblk[...] = jnp.zeros((S, 8, 128), F32)
-        for p in range(S):
-            r.sblk[p, :, 0:DR] = r.small[:, p * DR : (p + 1) * DR]
-
-        def send_small(i, carry):
-            p = lax.rem(s + i, S)
-            remote(r.sblk.at[p], r.srec.at[s], r.sm_s.at[0], r.sm_s.at[1], p, m).start()
-            return carry
-
-        lax.fori_loop(1, S, send_small, 0)
-        r.srec[s] = r.sblk[s]
-        sum_z("up")
+
+        def in_wait():
+            pass
+            sum_mid("down")
+            sum_z("up")
+
+        spread_end(in_wait)
         sum_far("qkv")
         sum_far("proj")
 
@@ -916,6 +998,18 @@
         mlp_start("r", 2, nt(r.dprer[...], r.wu[0]))
         routed_start("down", dmlp, r.actr[...])
         routed_start("up", r.n2r[...], r.dprer[...])
+        r.small[3:8] = jnp.zeros((5, D), F32)
+        r.sblk[...] = jnp.zeros((S, 8, 128), F32)
+        for p in range(S):
+            r.sblk[p, :, 0:DR] = r.small[:, p * DR : (p + 1) * DR]
+
+        def send_small(i, carry):
+            p = lax.rem(s + i, S)
+            remote(r.sblk.at[p], r.srec.at[s], r.sm_s.at[0], r.sm_s.at[1], p, m).start()
+            return carry
+
+        lax.fori_loop(1, S, send_small, 0)
+        r.srec[s] = r.sblk[s]
         dn, dg2 = rms_back(mlp_total("r", 2), r.attr[...], r.gains[0, 1:2])
         r.attr[...] = dn
         r.dattr[...] = (dmlp.astype(F32) + dn).astype(BF)
@@ -925,6 +1019,7 @@
         for copy in swaps:
             copy.start()
         routed_start("proj", r.dattr[...], r.mixr[...])
+        sum_mid("up")
         sum_z("qkv")
         sum_z("proj")
         dq_r[...] = jnp.zeros((H, RH, HD), F32)
@@ -962,7 +1057,8 @@
         mlp_start("r", 3, front_back(r.g3r, 0))
         routed_start("qkv", r.nr[...], r.g3r[...])
         sum_end("down")
-        sum_end("up")
+        sum_mid("qkv")
+        sum_mid("proj")
         dn, dg1 = rms_back(mlp_total("r", 3), r.chh[...].astype(F32), r.gains[0, 0:1])
         r.chg[gi] = (r.attr[...] + dn).astype(BF)
         r.gr[gi] = jnp.concatenate([dg1, dg2, jnp.zeros((6, D), F32)], axis=0)
@@ -984,6 +1080,7 @@
         r.sm_o[...] = jnp.sum(r.srec[...], axis=0)
         for k in KINDS:
             routed_end(k)
+        sum_end("up")
         sum_end("qkv")
         sum_end("proj")
         for item in (keys_all, query_all, grad_all, stat_all):

time: 171 us -> 161 us (0.942)
  Pallas kernels: 170 us -> 160 us
    pallas_call x1, Pallas kernels: 166 us -> 156 us  [run(): pl.pallas_call(kernel, out_shape=[jax.ShapeDtypeStruct(sh, dt) for sh, dt...]
where the time goes in v4:
time: 161 us
  Pallas kernels  160 us (99%)
    pallas_call x1, Pallas kernels, run(): pl.pallas_call(kernel, out_shape=[jax.ShapeDtypeStruct(sh, dt) for sh, dt...  156 us
    pallas_call x1, Pallas kernels, run(): pl.pallas_call(layout, out_shape=[jax.ShapeDtypeStruct(sh, dt) for sh, dt...  3.98 us

profile of v4, /device:TPU:0, one launch (start us, length us, event | category | flops | bytes accessed | tf_op | source)
XLA Modules:
  0.0 160.5 jit_solution(1713319772659531099)
XLA Ops:
  0.6 155.7 %train_step.1 = (bf16[128,768]{1,0:T(8,128)(2,1)}, bf16[128,768]{1,0:T(8,128)(2,1)}, f32[128,768]{1,0:T(8,128)}, f32[8,128]{1,0:T(8,128)}, f32[2,768]{1,0:T(2,12...) custom-call(bf16[128,768]{1,0:T(8,128)(2,1)} %refs_0_.1, ...), custom_call_target="tpu_custom_call" | custom-call | tf_op jit(solution)/shard_map/train_step/pallas_call | solution.py:1132
  156.4 4.0 %layout.1 = (bf16[128,768]{1,0:T(8,128)(2,1)}, bf16[128,768]{1,0:T(8,128)(2,1)}, f32[128,768]{1,0:T(8,128)}, f32[2,2,48]{2,1,0:T(2,128)}, f32[1,48]{1,0:T(1,128)...) custom-call(bf16[128,768]{1,0:T(8,128)(2,1)} %get-tuple-element.27.refs_0, ...), custom_call_target="tpu_custom_call" | custom-call | tf_op jit(solution)/shard_map/layout/pallas_call | solution.py:1154

commit v5 on v4

--- a/solution.py
+++ b/solution.py
@@ -22,6 +22,7 @@
 WIDE = 1536
 KV_CHAIN = True
 DO_CHAIN = False
+REDONE = ("down", "up")
 KINDS = ("down", "up", "proj", "qkv")
 
 
@@ -147,7 +148,8 @@
         "sel": ((T, D), BF),
         "ro": ((T, D), F32),
         "nd": ((T, D), BF),
-        "kva": ((S, T, 2 * W), BF),
+        "kall": ((S, T, W), BF),
+        "vall": ((S, T, W), BF),
         "qa": ((S, T, W), BF),
         "da": ((S, T, W), BF),
         "sta": ((S, 16, T), F32),
@@ -157,6 +159,8 @@
         "hid": ((T, D), F32),
         "n2d": ((T, D), BF),
         "dact": ((T, F), F32),
+        "nbr": ((2, Y - 1, T, D), BF),
+        "dactn": ((Y - 1, T, F), F32),
         "dattn": ((T, D), BF),
         "dq": ((H, max(T, RH), HD), F32),
         "dk": ((H, max(T, RH), HD), F32),
@@ -176,7 +180,8 @@
     for k in KINDS:
         X = XW[k]
         vm["left_" + k] = ((LEVEL, T, QY), BF)
-        vm["away_" + k] = ((Y - 1, T, QY), BF)
+        if k not in REDONE:
+            vm["away_" + k] = ((Y - 1, T, QY), BF)
         vm["right_" + k] = ((LEVEL, T, X), BF)
         vm["zsend_" + k] = ((Z, DRP, X), BF)
         vm["zown_" + k] = ((DRP, X), F32)
@@ -196,8 +201,10 @@
         "xd_r": (3, n - 1),
         "sw_s": (10, GN - 1),
         "sw_r": (10, GN - 1),
-        "kv_s": (n_sends,),
-        "kv_r": (S,),
+        "k_s": (n_sends,),
+        "k_r": (S,),
+        "v_s": (n_sends,),
+        "v_r": (S,),
         "q_s": (n_sends,),
         "q_r": (S,),
         "da_s": (n_sends,),
@@ -205,6 +212,8 @@
         "st_s": (n_sends,),
         "st_r": (S,),
         "sm_s": (2,),
+        "gn_s": (2, Y - 1),
+        "gn_r": (2, Y - 1),
         "gl_s": (4, 2, 2 * Y - 1),
         "gl_r": (4, 2, LEVEL),
         "gz_s": (4, Z - 1),
@@ -565,7 +574,7 @@
         def own_copies(k, side):
             mine = g[("left_", "right_")[side] + k].at[lev]
             out = [level_copy(k, side, 0, mine, lev, sib)]
-            for dy in range(1, Y):
+            for dy in range(1, 1 if k in REDONE else Y):
                 src = g["away_" + k].at[dy - 1] if side == 0 else mine
                 out.append(level_copy(k, side, dy, src, lev, rank(z, lax.rem(y + dy, Y), c)))
             return out
@@ -584,7 +593,7 @@
 
         def sum_left(k, lhs):
             g["left_" + k][lev] = nn(lhs[...], r.sele[y]).astype(BF)
-            for dy in range(1, Y):
+            for dy in range(1, 1 if k in REDONE else Y):
                 g["away_" + k][dy - 1] = nn(lhs[...], r.sele[lax.rem(y + dy, Y)]).astype(BF)
             for copy in own_copies(k, 0):
                 copy.start()
@@ -593,7 +602,39 @@
             for copy in own_copies(k, 1):
                 copy.start()
 
+        def give(i, src):
+            return [
+                remote(
+                    src, r.nbr.at[i, dy - 1], r.gn_s.at[i, dy - 1], r.gn_r.at[i, dy - 1], rank(z, lax.rem(y + dy, Y), c), m
+                )
+                for dy in range(1, Y)
+            ]
+
+        def redo_first():
+            for dy in range(1, Y):
+                give(0, r.cot)[dy - 1].wait_recv()
+                for x, w in chunks(F):
+                    r.dactn[dy - 1, :, x : x + w] = nt(r.nbr[0, dy - 1], r.wd[1, x : x + w, :])
+
+        def redo():
+            for dy in range(1, Y):
+                give(1, r.n2d)[dy - 1].wait_recv()
+                slot = level_slot(Y - dy, c)
+                for x, w in chunks(F):
+                    active, slope = gelu_pair(nn(r.nbr[1, dy - 1], r.wu[1, :, x : x + w]))
+                    r.right_down[slot, :, x : x + w] = active.astype(BF)
+                    r.right_up[slot, :, x : x + w] = (r.dactn[dy - 1, :, x : x + w] * slope).astype(BF)
+                r.left_down[slot] = nn(r.nbr[0, dy - 1], r.sele[y]).astype(BF)
+                r.left_up[slot] = nn(r.nbr[1, dy - 1], r.sele[y]).astype(BF)
+            for k in REDONE:
+                for copy in far_copies(k):
+                    copy.start()
+
         def sum_far(k):
+            if k in REDONE:
+                if k == REDONE[0]:
+                    redo()
+                return
             for dy in range(1, Y):
                 level_wait(k, level_slot(dy, c))
             for copy in far_copies(k):
@@ -817,6 +858,8 @@
         finish(r.mr, r.lr, r.ar, r.mixr)
         loads[1].wait()
         mlp_start("r", 0, nn(r.mixr[...], r.wp[0]))
+        for copy in give(0, r.cot):
+            copy.start()
         sum_left("down", r.cot)
         loads[2].wait()
         loads[3].wait()
@@ -829,6 +872,10 @@
             r.prer[:, x : x + w] = pre
             r.actr[:, x : x + w] = gelu_pair(pre)[0].astype(BF)
         mlp_start("r", 1, nn(r.actr[...], r.wd[0]))
+        for load in loads[4:]:
+            load.wait()
+        for x, w in chunks(F):
+            r.dact[:, x : x + w] = nt(r.cot[...], r.wd[1, x : x + w, :])
         mlp = mlp_total("r", 1)
         r.chg[gi] = (r.attr[...] + mlp).astype(BF)
         swaps = share(0, r.chg)
@@ -836,8 +883,6 @@
             copy.start()
         inp = r.inp[...].astype(F32)
         gate = jax.nn.sigmoid(jnp.sum(inp * r.router[...].reshape(1, D), axis=-1, keepdims=True))
-        for load in loads[4:]:
-            load.wait()
         for copy in swaps:
             copy.wait()
 
@@ -848,14 +893,17 @@
         r.ro_o[...] = ro.astype(BF)
         normed = rms(ro, r.gains[1, 0:1]).astype(BF)
         r.nd[...] = normed
-        r.kva[s, :, 0:W] = nn(normed, r.wq[1, 1]).astype(BF)
-        r.kva[s, :, W : 2 * W] = nn(normed, r.wq[1, 2]).astype(BF)
-        keys_all = gather(r.kva, r.kv_s, r.kv_r, True, KV_CHAIN)
+        r.kall[s] = nn(normed, r.wq[1, 1]).astype(BF)
+        r.vall[s] = nn(normed, r.wq[1, 2]).astype(BF)
+        keys_all = gather(r.kall, r.k_s, r.k_r, True, KV_CHAIN)
+        values_all = gather(r.vall, r.v_s, r.v_r, True, KV_CHAIN)
         keys_all.start()
+        values_all.start()
         r.qa[s] = (nn(normed, r.wq[1, 0]).astype(BF) * SCALE).astype(BF)
         query_all = gather(r.qa, r.q_s, r.q_r, False, False)
         query_all.start()
         keys_all.level()
+        values_all.level()
         query_all.level()
 
         def level_rows(ref, first=0):
@@ -879,12 +927,12 @@
 
         attend_start(r.md, r.ld, r.ad)
         walk(
-            [keys_all],
+            [keys_all, values_all],
             lambda dz: attend(
                 z - dz,
                 lambda h: r.qa[s, :, head(h)],
-                level_rows(r.kva),
-                level_rows(r.kva, H),
+                level_rows(r.kall),
+                level_rows(r.vall),
                 dense_mask,
                 r.md,
                 r.ld,
@@ -895,13 +943,14 @@
         mlp_start("d", 0, nn(r.right_proj[lev], r.wp[1]))
         loop(1, query_all.last + 1, query_all.z_step)
         sum_left("qkv", r.nd)
-        for x, w in chunks(F):
-            r.dact[:, x : x + w] = nt(r.cot[...], r.wd[1, x : x + w, :])
+        redo_first()
         attn = mlp_total("d", 0)
         hid = r.ro[...] + attn
         r.hid[...] = hid
         normed = rms(hid, r.gains[1, 1:2]).astype(BF)
         r.n2d[...] = normed
+        for copy in give(1, r.n2d):
+            copy.start()
         for x, w in chunks(F):
             active, slope = gelu_pair(nn(normed, r.wu[1, :, x : x + w]))
             r.right_down[lev, :, x : x + w] = active.astype(BF)
@@ -938,20 +987,22 @@
                 z - dz,
                 lambda h: r.qa[s, :, head(h)],
                 lambda h: r.da[s, :, head(h)],
-                level_rows(r.kva),
-                level_rows(r.kva, H),
+                level_rows(r.kall),
+                level_rows(r.vall),
                 dense_mask,
                 r.md,
                 r.ld,
                 dq_d,
             ),
         )
+        sum_far("down")
+        sum_far("up")
         walk(
             [grad_all, stat_all],
             lambda dz: back_keys(
                 z + dz,
-                lambda h: r.kva[s, :, head(h)],
-                lambda h: r.kva[s, :, head(H + h)],
+                lambda h: r.kall[s, :, head(h)],
+                lambda h: r.vall[s, :, head(h)],
                 level_rows(r.qa),
                 level_rows(r.da),
                 dense_mask_back,
@@ -960,8 +1011,6 @@
                 dv_d,
             ),
         )
-        sum_far("down")
-        sum_far("up")
         sum_z("down")
         pack_grads(dq_d, dk_d, dv_d, r.right_qkv.at[lev])
         mlp_start("d", 3, front_back(r.right_qkv.at[lev], 1))
@@ -1083,35 +1132,39 @@
         sum_end("up")
         sum_end("qkv")
         sum_end("proj")
-        for item in (keys_all, query_all, grad_all, stat_all):
+        for item in (keys_all, values_all, query_all, grad_all, stat_all):
             item.end()
         for k in KINDS:
             sum_sent(k)
+        for i, src in enumerate((r.cot, r.n2d)):
+            for copy in give(i, src):
+                copy.wait_send()
 
     def layout(*refs):
-        moved = [refs[i] for i in (0, 1, 2, 5, 6, 7, 8)]
-        sm, rg = refs[3:5]
-        moved_o = [refs[9 + i] for i in (0, 1, 2, 5, 6, 7, 8)]
-        gains_o, router_o = refs[12:14]
-        held, sems = refs[18:25], refs[25]
-        ways = [
-            (pltpu.make_async_copy(a, v, sems.at[0, i]), pltpu.make_async_copy(v, b, sems.at[1, i]))
-            for i, (a, v, b) in enumerate(zip(moved, held, moved_o))
-        ]
-        for into, _ in ways:
-            into.start()
+        into, out, held, made, sems = refs[:9], refs[9:18], refs[18:27], refs[27:29], refs[29]
+        order = (3, 4, 0, 1, 2, 5, 6, 7, 8)
+        reads = {i: pltpu.make_async_copy(into[i], held[i], sems.at[0, i]) for i in order}
+        for i in order:
+            reads[i].start()
+        made = {3: made[0], 4: made[1]}
+        writes = {i: pltpu.make_async_copy(made.get(i, held[i]), out[i], sems.at[1, i]) for i in order}
         s = lax.axis_index("seq")
+        reads[3].wait()
+        reads[4].wait()
+        sm, rg = held[3], held[4]
+        for i in order[2:]:
+            reads[i].wait()
+            writes[i].start()
         routed = rg[:, 0:DR]
         for p in range(1, S):
             routed = jnp.where(s == p, rg[:, p * DR : (p + 1) * DR], routed)
-        gains_o[0] = routed
-        gains_o[1] = sm[0:2, 0:DR]
-        router_o[...] = sm[2:3, 0:DR]
-        for into, out in ways:
-            into.wait()
-            out.start()
-        for _, out in ways:
-            out.wait()
+        made[3][0] = routed
+        made[3][1] = sm[0:2, 0:DR]
+        made[4][...] = sm[2:3, 0:DR]
+        writes[3].start()
+        writes[4].start()
+        for i in order:
+            writes[i].wait()
 
     def run(inp, segments, picks, gains, router, qkv, proj, up, down, cot):
         args = (
@@ -1154,9 +1207,11 @@
         last = pl.pallas_call(
             layout,
             out_shape=[jax.ShapeDtypeStruct(sh, dt) for sh, dt in shapes],
-            in_specs=[hbm] * 3 + [vmem] * 2 + [hbm] * 4,
-            out_specs=[hbm] * 3 + [vmem] * 2 + [hbm] * 4,
-            scratch_shapes=[pltpu.VMEM(*shapes[i]) for i in (0, 1, 2, 5, 6, 7, 8)] + [DMA((2, 7))],
+            in_specs=[hbm] * 9,
+            out_specs=[hbm] * 9,
+            scratch_shapes=[pltpu.VMEM(x.shape, x.dtype) for x in res]
+            + [pltpu.VMEM(*shapes[i]) for i in (3, 4)]
+            + [DMA((2, 9))],
             compiler_params=pltpu.CompilerParams(vmem_limit_bytes=62 * 1024 * 1024),
             name="layout",
         )(*res)

time: 161 us -> 159 us (0.988)
  Pallas kernels: 160 us -> 158 us
where the time goes in v5:
time: 159 us
  Pallas kernels  158 us (99%)
    pallas_call x1, Pallas kernels, run(): pl.pallas_call(kernel, out_shape=[jax.ShapeDtypeStruct(sh, dt) for sh, dt...  155 us
    pallas_call x1, Pallas kernels, run(): pl.pallas_call(layout, out_shape=[jax.ShapeDtypeStruct(sh, dt) for sh, dt...  3.61 us

profile of v5, /device:TPU:0, one launch (start us, length us, event | category | flops | bytes accessed | tf_op | source)
XLA Modules:
  0.0 159.1 jit_solution(11289822862668957892)
XLA Ops:
  0.6 154.7 %train_step.1 = (bf16[128,768]{1,0:T(8,128)(2,1)}, bf16[128,768]{1,0:T(8,128)(2,1)}, f32[128,768]{1,0:T(8,128)}, f32[8,128]{1,0:T(8,128)}, f32[2,768]{1,0:T(2,12...) custom-call(bf16[128,768]{1,0:T(8,128)(2,1)} %refs_0_.1, ...), custom_call_target="tpu_custom_call" | custom-call | tf_op jit(solution)/shard_map/train_step/pallas_call | solution.py:1185
  155.4 3.6 %layout.1 = (bf16[128,768]{1,0:T(8,128)(2,1)}, bf16[128,768]{1,0:T(8,128)(2,1)}, f32[128,768]{1,0:T(8,128)}, f32[2,2,48]{2,1,0:T(2,128)}, f32[1,48]{1,0:T(1,128)...) custom-call(bf16[128,768]{1,0:T(8,128)(2,1)} %get-tuple-element.27.refs_0, ...), custom_call_target="tpu_custom_call" | custom-call | tf_op jit(solution)/shard_map/layout/pallas_call | solution.py:1207

commit v6 on v5

--- a/solution.py
+++ b/solution.py
@@ -70,7 +70,7 @@
 
 
 def chunks(extent):
-    width = 384 if extent % 384 == 0 else extent
+    width = 768 if extent % 768 == 0 else 384 if extent % 384 == 0 else extent
     return [(at, width) for at in range(0, extent, width)]
 
 
@@ -361,7 +361,7 @@
             acc[...] = jnp.zeros(acc.shape, F32)
 
         def head_groups(width):
-            step = min(H, max(1, WIDE // width))
+            step = min(H, max(1, (2 * WIDE if CH <= 512 else WIDE) // width))
             return [range(at, min(at + step, H)) for at in range(0, H, step)]
 
         def attend(ci, query, key, value, mask, top, total, acc):

time: 159 us -> 159 us (level)
  no operation moved by 1% of the time
where the time goes in v6:
time: 159 us
  Pallas kernels  158 us (99%)
    pallas_call x1, Pallas kernels, run(): pl.pallas_call(kernel, out_shape=[jax.ShapeDtypeStruct(sh, dt) for sh, dt...  154 us
    pallas_call x1, Pallas kernels, run(): pl.pallas_call(layout, out_shape=[jax.ShapeDtypeStruct(sh, dt) for sh, dt...  3.61 us

profile of v6, /device:TPU:0, one launch (start us, length us, event | category | flops | bytes accessed | tf_op | source)
XLA Modules:
  0.0 158.9 jit_solution(4990663354213787493)
XLA Ops:
  0.6 154.5 %train_step.1 = (bf16[128,768]{1,0:T(8,128)(2,1)}, bf16[128,768]{1,0:T(8,128)(2,1)}, f32[128,768]{1,0:T(8,128)}, f32[8,128]{1,0:T(8,128)}, f32[2,768]{1,0:T(2,12...) custom-call(bf16[128,768]{1,0:T(8,128)(2,1)} %refs_0_.1, ...), custom_call_target="tpu_custom_call" | custom-call | tf_op jit(solution)/shard_map/train_step/pallas_call | solution.py:1185
  155.1 3.6 %layout.1 = (bf16[128,768]{1,0:T(8,128)(2,1)}, bf16[128,768]{1,0:T(8,128)(2,1)}, f32[128,768]{1,0:T(8,128)}, f32[2,2,48]{2,1,0:T(2,128)}, f32[1,48]{1,0:T(1,128)...) custom-call(bf16[128,768]{1,0:T(8,128)(2,1)} %get-tuple-element.27.refs_0, ...), custom_call_target="tpu_custom_call" | custom-call | tf_op jit(solution)/shard_map/layout/pallas_call | solution.py:1207
